TPU v7x, 512 devices: a whole 4x4x16 slice. The times are simulated.
512 devices in a mesh: slab: 64 (over y, x, z_hi, core), head: 8 (over z_lo).
Axes of the slice: x: 4, y: 4, z: 16 (z_hi: 2, z_lo: 8; z = z_hi * 8 + z_lo), core: 2. Of those that a mesh axis runs over, the one named last changes fastest.
Arguments:
- fresh_qkv: bfloat16 [3, 8192, 3072], P(None, ('slab', 'head')), may hold values from -6 to 6
- stale_kv: bfloat16 [2, 8192, 3072], P(None, 'slab', 'head'), may hold values from -6 to 6
- out_weight: bfloat16 [3072, 3072], P('head'), may hold values from -0.109375 to 0.109375
- branch_gate: float32 [3072], replicated, may hold values from 0.5 to 2
- residual: bfloat16 [8192, 3072], P(('slab', 'head')), may hold values from -6 to 6
Outputs:
- block_out: bfloat16 [8192, 3072], P(('slab', 'head'))
- next_kv: bfloat16 [2, 8192, 3072], P(None, 'slab', 'head')
All inputs are finite; a program needn't handle non-finite values.
Results may differ from a plain program's by a relative error of at most 0.014.
Values may be sent and summed in bfloat16 or wider, within the bound.
No kernel may reach another device: no remote copies, remote signals or barrier semaphores. Data moves between devices by JAX's collectives and lax.ppermute only.
A program may use at most 64 MiB of HBM per device.

v0:
```python
import math

import jax
import jax.numpy as jnp
from jax import lax
from jax.sharding import PartitionSpec as P

HEAD_DIM = 128


masked_score = -1e30


def fold_slabs(carry, kv_part, queries, own_start, slab_rows):
    row_top, row_total, summed = carry
    part_rows = kv_part.shape[1]
    score_scale = 1.0 / math.sqrt(HEAD_DIM)
    channel = lax.broadcasted_iota(jnp.int32, (1, part_rows), 1)
    own_cols = (channel >= own_start) & (channel < own_start + slab_rows)

    def per_head(items):
        head_no, top_head, total_head, summed_head = items
        query_head = queries[head_no]
        key_head = lax.dynamic_slice_in_dim(kv_part[0], head_no * HEAD_DIM, HEAD_DIM, 1)
        value_head = lax.dynamic_slice_in_dim(kv_part[1], head_no * HEAD_DIM, HEAD_DIM, 1)
        scores = (
            lax.dot_general(
                query_head, key_head, (((1,), (1,)), ((), ())), preferred_element_type=jnp.float32
            )
            * score_scale
        )
        scores = jnp.where(own_cols, masked_score, scores)
        new_top = jnp.maximum(top_head, jnp.max(scores, axis=1))
        rescale = jnp.exp(top_head - new_top)
        weights_f = jnp.exp(scores - new_top[:, None])
        new_total = total_head * rescale + jnp.sum(weights_f, axis=1)
        new_summed = summed_head * rescale[:, None] + jnp.dot(
            weights_f.astype(jnp.bfloat16), value_head, preferred_element_type=jnp.float32
        )
        return (new_top, new_total, new_summed)

    head_ids = jnp.arange(queries.shape[0], dtype=jnp.int32)
    return lax.map(per_head, (head_ids, row_top, row_total, summed))


def local(fresh_qkv, stale_kv, out_weight, branch_gate, residual):
    headwise = lax.all_to_all(fresh_qkv, "head", split_axis=2, concat_axis=1, tiled=True)
    slab_rows = headwise.shape[1]
    heads_here = headwise.shape[2] // HEAD_DIM
    score_scale = 1.0 / math.sqrt(HEAD_DIM)
    queries = jnp.transpose(headwise[0].reshape(slab_rows, heads_here, HEAD_DIM), (1, 0, 2))
    fresh_keys = jnp.transpose(headwise[1].reshape(slab_rows, heads_here, HEAD_DIM), (1, 0, 2))
    fresh_values = jnp.transpose(headwise[2].reshape(slab_rows, heads_here, HEAD_DIM), (1, 0, 2))
    slab_index = lax.axis_index("slab")
    own_start = slab_index * slab_rows
    own_scores = (
        jnp.einsum("hqd,hkd->hqk", queries, fresh_keys, preferred_element_type=jnp.float32)
        * score_scale
    )
    first_top = jnp.max(own_scores, axis=2)
    own_weights = jnp.exp(own_scores - first_top[:, :, None])
    first_total = jnp.sum(own_weights, axis=2)
    first_summed = jnp.einsum(
        "hqk,hkd->hqd",
        own_weights.astype(jnp.bfloat16),
        fresh_values,
        preferred_element_type=jnp.float32,
    )
    initial = (first_top, first_total, first_summed)
    gathered = lax.all_gather(stale_kv, "slab", axis=1, tiled=True)
    row_top, row_total, summed = fold_slabs(initial, gathered, queries, own_start, slab_rows)
    attended = summed / row_total[:, :, None]
    attended = (
        jnp.transpose(attended, (1, 0, 2))
        .reshape(slab_rows, heads_here * HEAD_DIM)
        .astype(jnp.bfloat16)
    )
    projected = lax.psum_scatter(
        jnp.dot(attended, out_weight, preferred_element_type=jnp.float32).astype(jnp.bfloat16),
        "head",
        scatter_dimension=0,
        tiled=True,
    ).astype(jnp.float32)
    block_out = (residual.astype(jnp.float32) + branch_gate[None, :] * projected).astype(
        jnp.bfloat16
    )
    next_kv = headwise[1:3]
    return (block_out, next_kv)


def solution(mesh):
    placed = (
        P(None, ("slab", "head"), None),
        P(None, "slab", "head"),
        P("head", None),
        P(),
        P(("slab", "head"), None),
    )
    return jax.shard_map(
        local,
        mesh=mesh,
        in_specs=placed,
        out_specs=(P(("slab", "head"), None), P(None, "slab", "head")),
        check_vma=False,
    )
```

profile of v0, /device:TPU:1, one launch (start us, length us, event | category | flops | bytes accessed | tf_op | source)
XLA Modules:
  0.0 334.0 jit_solution(3271969961414770308)
XLA Ops:
  7.9 4.4 %copy.15 = bf16[3,16,3072]{1,0,2:T(4,128)(2,1)} copy(bf16[3,16,3072]{2,1,0:T(8,128)(2,1)} %param.7) | data formatting | bytes 589824 | tf_op args[0]
  12.3 5.0 %reshape.58 = bf16[8,2,9216]{2,1,0:T(2,128)(2,1)} reshape(bf16[3072,3,16]{2,1,0:T(4,128)(2,1)} %bitcast.83) | data formatting | bytes 589824
  17.3 13.1 %all-to-all-start = ((bf16[8,2,9216]{2,1,0:T(2,128)(2,1)}), bf16[8,2,9216]{2,1,0:T(2,128)(2,1)S(1)}, u32[]{:S(2)}, u32[]{:S(2)}) async-start(bf16[8,2,9216]{2,1,0:T(2,128)(2,1)} %reshape.58), calls=%async_computation | async-start | bytes 589824 | tf_op jit(solution)/shard_map/all_to_all | solution.py:47
  30.4 14.8 %all-to-all-done = bf16[8,2,9216]{2,1,0:T(2,128)(2,1)S(1)} async-done(((bf16[8,2,9216]{2,1,0:T(2,128)(2,1)}), bf16[8,2,9216]{2,1,0:T(2,128)(2,1)S(1)}, u32[]{:S(2)}, u32[]{:S(2)}) %all-to-all-start) | async-done | bytes 294944 | tf_op jit(solution)/shard_map/all_to_all | solution.py:47
  45.3 4.1 %reshape.59 = bf16[3072,3,16]{2,1,0:T(4,128)(2,1)} reshape(bf16[8,2,9216]{2,1,0:T(2,128)(2,1)S(1)} %all-to-all-done) | data formatting | bytes 589824
  49.3 4.1 %copy.16 = bf16[3,16,8,384]{3,1,2,0:T(8,128)(2,1)S(1)} copy(bf16[3,16,8,384]{1,0,3,2:T(4,128)(2,1)} %bitcast.82) | data formatting | bytes 589824 | tf_op jit(solution)/shard_map/all_to_all | solution.py:47
  54.1 183.3 %all-gather.2.cloned.1.call-done = bf16[2,8192,384]{2,1,0:T(8,128)(2,1)} async-done(((bf16[2,128,384]{2,1,0:T(8,128)(2,1)}), bf16[2,8192,384]{2,1,0:T(8,128)(2,1)}) %all-gather.2.cloned.1.call-update) | async-done | bytes 12582928 | tf_op jit(solution)/shard_map/all_gather | solution.py:70
  237.4 36.1 %while.13 = (s32[]{:T(128)}, f32[3,128]{1,0:T(4,128)S(1)}, f32[3,128,128]{1,2,0:T(8,128)S(1)}, f32[3,128]{1,0:T(4,128)S(1)}, f32[3,128]{1,0:T(4,128)S(1)}, /*ind...) while((s32[]{:T(128)}, f32[3,128]{1,0:T(4,128)S(1)}, ...), condition=%wide.region_5.6_spmd.clone, body=%wide.region_2.5_spmd.clone.sunk | while | flops 544268800 | bytes 42393884 | solution.py:43
  240.6 6.0 %fusion.54 = (bf16[1,8192,384]{2,1,0:T(8,128)(2,1)S(1)}, bf16[1,8192,384]{2,1,0:T(8,128)(2,1)S(1)}) fusion(bf16[2,8192,384]{2,1,0:T(8,128)(2,1)} %get-tuple-element.234), kind=kLoop, calls=%fused_computation.44.clone.1 | loop fusion | bytes 25165824 | tf_op jit(solution)/shard_map/while/body/eval_jaxpr/slice | solution.py:25
  246.6 0.9 fusion.55
  247.6 0.9 fusion.58
  248.5 0.8 fusion.57
  252.6 6.0 %fusion.54 = (bf16[1,8192,384]{2,1,0:T(8,128)(2,1)S(1)}, bf16[1,8192,384]{2,1,0:T(8,128)(2,1)S(1)}) fusion(bf16[2,8192,384]{2,1,0:T(8,128)(2,1)} %get-tuple-element.234), kind=kLoop, calls=%fused_computation.44.clone.1 | loop fusion | bytes 25165824 | tf_op jit(solution)/shard_map/while/body/eval_jaxpr/slice | solution.py:25
  258.7 0.9 fusion.55
  259.6 0.9 fusion.58
  260.6 0.8 fusion.57
  264.7 6.0 %fusion.54 = (bf16[1,8192,384]{2,1,0:T(8,128)(2,1)S(1)}, bf16[1,8192,384]{2,1,0:T(8,128)(2,1)S(1)}) fusion(bf16[2,8192,384]{2,1,0:T(8,128)(2,1)} %get-tuple-element.234), kind=kLoop, calls=%fused_computation.44.clone.1 | loop fusion | bytes 25165824 | tf_op jit(solution)/shard_map/while/body/eval_jaxpr/slice | solution.py:25
  270.7 0.9 fusion.55
  271.7 0.9 fusion.58
  272.6 0.8 fusion.57
  273.6 1.5 convolution_convert_fusion
  275.1 0.7 slice.34
  275.8 49.7 %reduce-scatter.2.cloned.1.call-done = bf16[16,3072]{1,0:T(8,128)(2,1)} async-done(((bf16[128,3072]{1,0:T(8,128)(2,1)}), bf16[16,3072]{1,0:T(8,128)(2,1)}) %reduce-scatter.2.cloned.1.call-update) | async-done | bytes 98320 | tf_op jit(solution)/shard_map/reduce_scatter | solution.py:78
  325.5 1.6 add_convert_fusion
  (43 shorter events, 4.2 us)
Async XLA Ops:
  7.2 266.4 %copy-start = (bf16[384,3072]{1,0:T(8,128)(2,1)S(1)}, bf16[384,3072]{1,0:T(8,128)(2,1)}, u32[]{:S(2)}) copy-start(bf16[384,3072]{1,0:T(8,128)(2,1)} %param.9) | copy-start | bytes 7077892
  7.2 230.2 %all-gather.2.cloned.1.call-start = ((), (), s32[]{:S(2)}) async-start(), calls=%async_computation.2 | async-start | bytes 12779520 | tf_op jit(solution)/shard_map/all_gather | solution.py:70
  17.3 28.0 %all-to-all-start = ((bf16[8,2,9216]{2,1,0:T(2,128)(2,1)}), bf16[8,2,9216]{2,1,0:T(2,128)(2,1)S(1)}, u32[]{:S(2)}, u32[]{:S(2)}) async-start(bf16[8,2,9216]{2,1,0:T(2,128)(2,1)} %reshape.58), calls=%async_computation | async-start | bytes 589824 | tf_op jit(solution)/shard_map/all_to_all | solution.py:47
  30.3 295.2 %reduce-scatter.2.cloned.1.call-start = ((), (), s32[]{:S(2)}) async-start(), calls=%async_computation.3 | async-start | bytes 884736 | tf_op jit(solution)/shard_map/reduce_scatter | solution.py:78
  273.5 52.0 %copy-start.1 = (bf16[16,3072]{1,0:T(8,128)(2,1)S(1)}, bf16[16,3072]{1,0:T(8,128)(2,1)}, u32[]{:S(2)}) copy-start(bf16[16,3072]{1,0:T(8,128)(2,1)} %param.11) | copy-start | bytes 294916
  273.6 52.0 %copy-start.2 = (f32[3072]{0:T(1024)S(1)}, f32[3072]{0:T(1024)}, u32[]{:S(2)}) copy-start(f32[3072]{0:T(1024)} %param.10) | copy-start | bytes 36868
Sparse Core Ops, SparseCore 0:
  12.5 224.8 all-gather.1
  275.2 50.2 reduce-scatter.1
where the time goes:
time: 339 us; the launch traced here: 334 us
  waiting for transfers between devices  249 us (73%)
  local copies, waits for them, and re-layouts  38.8 us (11%)
  between operations  14.2 us (4%)
  starting transfers between devices  13.2 us (4%)
  matrix products  7.51 us (2%)
  loops' own time  7.43 us (2%)
  other arithmetic  4.39 us (1%)
    all_gather x1, waiting for transfers between devices, local(): gathered = lax.all_gather(stale_kv, 'slab', axis=1, tiled=True)  183 us
    reduce_scatter x1, waiting for transfers between devices, local(): lax.psum_scatter(jnp.dot(attended, out_weight, preferred_element_type=jnp...  49.7 us
    slice x3, local copies, waits for them, and re-layouts, per_head(): kv_part[1]  18.1 us
    all_to_all x1, waiting for transfers between devices, local(): lax.all_to_all(fresh_qkv, 'head', split_axis=2, concat_axis=1, tiled=True)  14.8 us
    unnamed x9, local copies, waits for them, and re-layouts  13.5 us
    all_to_all x1, starting transfers between devices, local(): lax.all_to_all(fresh_qkv, 'head', split_axis=2, concat_axis=1, tiled=True)  13.1 us
    another operation x1, loops' own time, fold_slabs(): return lax.map(per_head, (head_ids, row_top, row_total, summed))  7.43 us
  transfers between devices with their start and end apart: 3, of which 3 were waited for; matrix products, arithmetic and copies ran while one was open for 6% of the time, Pallas kernels for 0%

commit v1 on v0

v1 whole, which is shorter than its diff:
```python
import functools
import math

import jax
import jax.numpy as jnp
from jax import lax
from jax.experimental import pallas as pl
from jax.experimental.pallas import tpu as pltpu
from jax.sharding import Mesh, PartitionSpec as P

HEAD_DIM = 128
AXES = ("yh", "yl", "x", "zh", "core", "head")
SLAB_AXES = AXES[:-1]
SIZES = (2, 2, 4, 2, 2, 8)
KEY_AXES = ("yh", "x")
N_HEAD = 8
HEADS_HERE = 3
WIDTH = HEADS_HERE * HEAD_DIM
SLAB = 128
PIECE = SLAB // N_HEAD
D = N_HEAD * WIDTH
KEY_SLABS = 8
KEYS = KEY_SLABS * SLAB
PAIR = 2 * SLAB
STAT_ROWS = 16
ROWS = WIDTH + STAT_ROWS
LOG2E = 1.4426950408889634
FACTOR = LOG2E / math.sqrt(HEAD_DIM)
MASKED = -1e30
PIECE_ORDER = (0, 4, 2, 6, 1, 5, 3, 7)

VMEM = pl.BlockSpec(memory_space=pltpu.VMEM)
SMEM = pl.BlockSpec(memory_space=pltpu.SMEM)
ANY = pl.BlockSpec(memory_space=pl.ANY)
BF16 = jnp.bfloat16
F32 = jnp.float32


def swap(n, bit):
    return [(i, i ^ bit) for i in range(n)]


def call(body, out_shape, n_in, scratch=(), in_specs=None, flops=0, vmem=None, name=None):
    out_specs = jax.tree.map(lambda _: VMEM, out_shape)
    return pl.pallas_call(
        body,
        out_shape=out_shape,
        in_specs=in_specs or [VMEM] * n_in,
        out_specs=out_specs,
        scratch_shapes=list(scratch),
        compiler_params=pltpu.CompilerParams(vmem_limit_bytes=vmem or (32 << 20)),
        cost_estimate=pl.CostEstimate(flops=flops, bytes_accessed=1 << 19, transcendentals=0),
        name=name,
    )


def shape(dims, dtype):
    return jax.ShapeDtypeStruct(dims, dtype)


def pack_q_body(fresh_ref, out_ref):
    for h in range(N_HEAD):
        piece = fresh_ref[0, :, h * WIDTH : (h + 1) * WIDTH]
        out_ref[h] = piece
        out_ref[N_HEAD + h] = piece


def pack_kv_body(fresh_ref, after_ref, out_ref):
    del after_ref
    for h in range(N_HEAD):
        for part in range(2):
            out_ref[h, part] = fresh_ref[1 + part, :, h * WIDTH : (h + 1) * WIDTH]


def stat_rows(lses):
    n = lses[0].shape[1]
    high = [v.astype(BF16).astype(F32) for v in lses]
    rest = [v - w for v, w in zip(lses, high)]
    mid = [v.astype(BF16).astype(F32) for v in rest]
    low = [v - w for v, w in zip(rest, mid)]
    pad = jnp.zeros((STAT_ROWS - 3 * HEADS_HERE, n), F32)
    return jnp.concatenate(high + mid + low + [pad], axis=0).astype(BF16)


def read_stats(rows):
    rows = rows.astype(F32)
    n = HEADS_HERE
    return [rows[h : h + 1] + rows[n + h : n + h + 1] + rows[2 * n + h : 2 * n + h + 1] for h in range(n)]


def soft(s, values_t):
    top = jnp.max(s, axis=0, keepdims=True)
    weights = jnp.exp2((s - top) * FACTOR)
    total = jnp.sum(weights, axis=0, keepdims=True)
    summed = jnp.dot(values_t, weights.astype(BF16), preferred_element_type=F32)
    return summed / total, top * FACTOR + jnp.log2(total)


def scores_of(keys, queries):
    return lax.dot_general(keys, queries, (((1,), (1,)), ((), ())), preferred_element_type=F32)


def attend_body(own_first, pos_ref, qa_ref, qb_ref, kv_ref, oa_ref, ob_ref, s_ref):
    lses = [[], []]
    for h in range(HEADS_HERE):
        cols = slice(h * HEAD_DIM, (h + 1) * HEAD_DIM)
        keys = kv_ref[:, 0, :, cols].reshape(KEYS, HEAD_DIM)
        values_t = kv_ref[:, 1, :, cols].reshape(KEYS, HEAD_DIM).T
        for i, (q_ref, o_ref) in enumerate(((qa_ref, oa_ref), (qb_ref, ob_ref))):
            s_ref[i] = scores_of(keys, q_ref[:, cols])
            if own_first and i == 0:
                first = pl.multiple_of(pos_ref[0] * SLAB, SLAB)
                lane = pl.multiple_of(pos_ref[1] * SLAB, SLAB)
                s_ref[0, pl.ds(first, SLAB), pl.ds(lane, SLAB)] = jnp.full((SLAB, SLAB), MASKED, F32)
            out, lse = soft(s_ref[i], values_t)
            o_ref[h * HEAD_DIM : (h + 1) * HEAD_DIM] = out.astype(BF16)
            lses[i].append(lse)
    oa_ref[WIDTH:] = stat_rows(lses[0])
    ob_ref[WIDTH:] = stat_rows(lses[1])


def attend(own_first, pos, qa, qb, kv):
    return call(
        functools.partial(attend_body, own_first),
        (shape((ROWS, PAIR), BF16), shape((ROWS, PAIR), BF16)),
        4,
        scratch=[pltpu.VMEM((2, KEYS, PAIR), F32)],
        in_specs=[SMEM, VMEM, VMEM, VMEM],
        flops=4 * HEADS_HERE * KEYS * 2 * PAIR * HEAD_DIM,
        name="attend",
    )(pos, qa, qb, kv)


def own_body(pos_ref, q_ref, fresh_ref, out_ref, next_ref):
    for piece in range(N_HEAD):
        for part in range(2):
            next_ref[part, piece * PIECE : (piece + 1) * PIECE] = fresh_ref[piece, part]
    row = pl.multiple_of(pos_ref[1] * SLAB, SLAB)
    lses = []
    for h in range(HEADS_HERE):
        cols = slice(h * HEAD_DIM, (h + 1) * HEAD_DIM)
        s = scores_of(next_ref[0, :, cols], q_ref[pl.ds(row, SLAB), cols])
        out, lse = soft(s, next_ref[1, :, cols].T)
        out_ref[h * HEAD_DIM : (h + 1) * HEAD_DIM] = out
        lses.append(lse)
    out_ref[WIDTH:] = jnp.concatenate(lses + [jnp.zeros((8 - HEADS_HERE, SLAB), F32)], axis=0)


def merge(outs, lses):
    top = functools.reduce(jnp.maximum, lses)
    shares = [jnp.exp2(v - top) for v in lses]
    total = sum(shares)
    merged = sum(o.astype(F32) * (w / total) for o, w in zip(outs, shares))
    return merged, top + jnp.log2(total)


def merge_to_bf16(parts, out_ref):
    stats = [read_stats(p[WIDTH:]) for p in parts]
    lses = []
    for h in range(HEADS_HERE):
        rows = slice(h * HEAD_DIM, (h + 1) * HEAD_DIM)
        out, lse = merge([p[rows] for p in parts], [v[h] for v in stats])
        out_ref[rows] = out.astype(BF16)
        lses.append(lse)
    out_ref[WIDTH:] = stat_rows(lses)


def merge_two_body(a_ref, b_ref, out_ref):
    merge_to_bf16([a_ref, b_ref], out_ref)


def merge_three_body(pos_ref, a_ref, b_ref, c_ref, keep_ref, send_ref):
    here = pl.multiple_of(pos_ref[1] * SLAB, SLAB)
    there = pl.multiple_of((1 - pos_ref[1]) * SLAB, SLAB)
    refs = (a_ref, b_ref, c_ref)
    merge_to_bf16([r.at[:, pl.ds(there, SLAB)] for r in refs], send_ref)
    parts = [r.at[:, pl.ds(here, SLAB)] for r in refs]
    stats = [read_stats(p[WIDTH:]) for p in parts]
    lses = []
    for h in range(HEADS_HERE):
        rows = slice(h * HEAD_DIM, (h + 1) * HEAD_DIM)
        out, lse = merge([p[rows] for p in parts], [v[h] for v in stats])
        keep_ref[rows] = out
        lses.append(lse)
    keep_ref[WIDTH:] = jnp.concatenate(lses + [jnp.zeros((8 - HEADS_HERE, SLAB), F32)], axis=0)


def project_body(pos_ref, keep_ref, other_ref, own_ref, w_ref, keep_out, send_out, att_ref, proj_ref):
    other = read_stats(other_ref[WIDTH:])
    for h in range(HEADS_HERE):
        rows = slice(h * HEAD_DIM, (h + 1) * HEAD_DIM)
        out, _ = merge(
            [keep_ref[rows], other_ref[rows], own_ref[rows]],
            [keep_ref[WIDTH + h : WIDTH + h + 1], other[h], own_ref[WIDTH + h : WIDTH + h + 1]],
        )
        att_ref[:, rows] = out.T.astype(BF16)
    proj = jnp.dot(att_ref[...], w_ref[...], preferred_element_type=F32)
    for at, piece in enumerate(PIECE_ORDER):
        proj_ref[at * PIECE : (at + 1) * PIECE] = proj[piece * PIECE : (piece + 1) * PIECE]
    half = SLAB // 2
    bit = pos_ref[2]
    keep_out[...] = proj_ref[pl.ds(pl.multiple_of(bit * half, half), half)]
    send_out[...] = proj_ref[pl.ds(pl.multiple_of((1 - bit) * half, half), half)].astype(BF16)


def local(fresh_qkv, stale_kv, out_weight, branch_gate, residual):
    head = lax.axis_index("head")
    zh = lax.axis_index("zh")
    pos = jnp.stack([lax.axis_index(KEY_AXES), zh, head % 2]).astype(jnp.int32)

    kv = lax.all_gather(stale_kv, KEY_AXES, axis=0, tiled=False)

    q_packed = call(pack_q_body, shape((2 * N_HEAD, PIECE, WIDTH), BF16), 1, name="pack_q")(fresh_qkv[0:1])
    q_all = lax.all_to_all(q_packed, ("zh", "head"), 0, 0, tiled=True)
    q0 = q_all.reshape(PAIR, WIDTH)
    q2 = lax.ppermute(q0, "core", swap(2, 1))
    q1 = lax.ppermute(q0, "yl", swap(2, 1))
    q3 = lax.ppermute(q1, "core", swap(2, 1))

    kv_packed = call(
        pack_kv_body, shape((N_HEAD, 2, PIECE, WIDTH), BF16), 2, in_specs=[VMEM, ANY], name="pack_kv"
    )(fresh_qkv, q_all)
    kv_fresh = lax.all_to_all(kv_packed, "head", 0, 0, tiled=True)

    m0, m2 = attend(True, pos, q0, q2, kv)
    m0_core = lax.ppermute(m2, "core", swap(2, 1))
    m1, m3 = attend(False, pos, q1, q3, kv)
    m1_core = lax.ppermute(m3, "core", swap(2, 1))
    m1_sum = call(merge_two_body, shape((ROWS, PAIR), BF16), 2, name="merge_two")(m1, m1_core)
    m0_y = lax.ppermute(m1_sum, "yl", swap(2, 1))

    own, next_kv = call(
        own_body,
        (shape((WIDTH + 8, SLAB), F32), shape((2, SLAB, WIDTH), BF16)),
        3,
        in_specs=[SMEM, VMEM, VMEM],
        name="own",
    )(pos, q0, kv_fresh)

    keep, send = call(
        merge_three_body,
        (shape((WIDTH + 8, SLAB), F32), shape((ROWS, SLAB), BF16)),
        4,
        in_specs=[SMEM, VMEM, VMEM, VMEM],
        name="merge_three",
    )(pos, m0, m0_core, m0_y)
    other = lax.ppermute(send, "zh", swap(2, 1))

    kept, sent = call(
        project_body,
        (shape((SLAB // 2, D), F32), shape((SLAB // 2, D), BF16)),
        5,
        scratch=[pltpu.VMEM((SLAB, WIDTH), BF16), pltpu.VMEM((SLAB, D), F32)],
        in_specs=[SMEM] + [VMEM] * 4,
        name="project",
    )(pos, keep, other, own, out_weight)

    for bit in (1, 2, 4):
        kept = kept + lax.ppermute(sent, "head", swap(N_HEAD, bit)).astype(F32)
        if bit < 4:
            rows = kept.shape[0] // 2
            mine = (head // (2 * bit)) % 2
            sent = lax.dynamic_slice_in_dim(kept, (1 - mine) * rows, rows, 0).astype(BF16)
            kept = lax.dynamic_slice_in_dim(kept, mine * rows, rows, 0)
    block_out = (residual.astype(F32) + branch_gate[None, :] * kept).astype(BF16)
    return block_out, next_kv


def solution(mesh):
    fine = Mesh(mesh.devices.reshape(SIZES), AXES)
    return jax.shard_map(
        local,
        mesh=fine,
        in_specs=(
            P(None, AXES, None),
            P(None, SLAB_AXES, "head"),
            P("head", None),
            P(),
            P(AXES, None),
        ),
        out_specs=(P(AXES, None), P(None, SLAB_AXES, "head")),
        check_vma=False,
    )
```

time: 339 us -> 182 us (0.54); the launches traced: 334 us -> 181 us
  waiting for transfers between devices: 249 us -> 52.7 us
  starting transfers between devices: 13.2 us -> 67 us
  local copies, waits for them, and re-layouts: 38.8 us -> 3.34 us
  blocking collectives: 0 us -> 28.1 us
  Pallas kernels: 0 us -> 15 us
  matrix products: 7.51 us -> 0 us
  loops' own time: 7.43 us -> 0 us
  other arithmetic: 4.39 us -> 0.86 us
    all_gather x1, waiting for transfers between devices: 183 us -> 21.5 us  [local(): kv = lax.all_gather(stale_kv, KEY_AXES, axis=0, tiled=False)]
    ppermute x0 -> x10, starting transfers between devices: none -> 61.5 us  [the longest x3 27.6 us: local(): kept = kept + lax.ppermute(sent, 'head', swap(N_HEAD, bit)).astype(F32)]
    reduce_scatter x1 -> x0, waiting for transfers between devices: 49.7 us -> none  [local(): lax.psum_scatter(jnp.dot(attended, out_weight, preferred_element_type=jnp...]
    ppermute x0 -> x10, waiting for transfers between devices: none -> 30.5 us  [the longest x3 20.4 us: local(): kept = kept + lax.ppermute(sent, 'head', swap(N_HEAD, bit)).astype(F32)]
    all_to_all x0 -> x1, blocking collectives: none -> 28.1 us  [local(): q_all = lax.all_to_all(q_packed, ('zh', 'head'), 0, 0, tiled=True)]
    slice x5 -> x1, local copies, waits for them, and re-layouts: 18.9 us -> 0.9 us  [local(): fresh_qkv[0:1]]
    pallas_call x0 -> x8, Pallas kernels: none -> 15 us  [the longest x2 9.76 us: attend(): call(functools.partial(attend_body, own_first), (shape((ROWS, PAIR), BF16...]
    all_to_all x1, waiting for transfers between devices: 14.8 us -> 0.01 us  [local(): kv_fresh = lax.all_to_all(kv_packed, 'head', 0, 0, tiled=True)]
  transfers between devices with their start and end apart: 3 -> 12, of which waited for: 3 -> 7; matrix products, arithmetic and copies ran while one was open for 6% -> 1% of each run, Pallas kernels for 0% -> 7%
where the time goes in v1:
time: 182 us; the launch traced here: 181 us
  starting transfers between devices  67 us (37%)
  waiting for transfers between devices  52.7 us (29%)
  blocking collectives  28.1 us (15%)
  Pallas kernels  15 us (8%)
  between operations  14.3 us (8%)
  local copies, waits for them, and re-layouts  3.34 us (2%)
    all_to_all x1, blocking collectives, local(): q_all = lax.all_to_all(q_packed, ('zh', 'head'), 0, 0, tiled=True)  28.1 us
    ppermute x3, starting transfers between devices, local(): kept = kept + lax.ppermute(sent, 'head', swap(N_HEAD, bit)).astype(F32)  27.6 us
    all_gather x1, waiting for transfers between devices, local(): kv = lax.all_gather(stale_kv, KEY_AXES, axis=0, tiled=False)  21.5 us
    ppermute x3, waiting for transfers between devices, local(): kept = kept + lax.ppermute(sent, 'head', swap(N_HEAD, bit)).astype(F32)  20.4 us
    ppermute x1, starting transfers between devices, local(): other = lax.ppermute(send, 'zh', swap(2, 1))  12.5 us
    pallas_call x2, Pallas kernels, attend(): call(functools.partial(attend_body, own_first), (shape((ROWS, PAIR), BF16...  9.76 us
    ppermute x1, starting transfers between devices, local(): q3 = lax.ppermute(q1, 'core', swap(2, 1))  7.48 us
    ppermute x1, waiting for transfers between devices, local(): m0_y = lax.ppermute(m1_sum, 'yl', swap(2, 1))  5.81 us
  transfers between devices with their start and end apart: 12, of which 7 were waited for; matrix products, arithmetic and copies ran while one was open for 1% of the time, Pallas kernels for 7%

profile of v1, /device:TPU:1, one launch (start us, length us, event | category | flops | bytes accessed | tf_op | source)
XLA Modules:
  0.0 181.4 jit_solution(17179668296729335773)
XLA Ops:
  8.8 28.1 %all_to_all.10.after_ref = bf16[16,16,384]{2,1,0:T(8,128)(2,1)S(1)} all-to-all(bf16[16,16,384]{2,1,0:T(8,128)(2,1)S(1)} %pack_q.1), channel_id=1, replica_groups=mesh['yh'=2,'yl'=2,'x'=4,'zh'=2,'core'=2,'head'=8] {'zh','head'}, dimensions={0} | all-to-all | bytes 393216 | tf_op jit(solution)/shard_map/all_to_all | solution.py:214
  36.9 3.2 %collective-permute-start.2 = (bf16[256,384]{1,0:T(8,128)(2,1)S(1)}, bf16[256,384]{1,0:T(8,128)(2,1)S(1)}, u32[]{:S(2)}, u32[]{:S(2)}) collective-permute-start(bf16[256,384]{1,0:T(8,128)(2,1)S(1)} %bitcast.5), channel_id=1, source_target_pairs={{0,128},{128,0},{1,129},{129,1},{2,130},{130,2},{3,131},{131,3},{4... | collective-permute-start | bytes 589832 | tf_op jit(solution)/shard_map/ppermute | solution.py:217
  40.1 3.6 %collective-permute-done.2.qa_ref = bf16[256,384]{1,0:T(8,128)(2,1)S(1)} collective-permute-done((bf16[256,384]{1,0:T(8,128)(2,1)S(1)}, bf16[256,384]{1,0:T(8,128)(2,1)S(1)}, u32[]{:S(2)}, u32[]{:S(2)}) %collective-permute-start.2) | collective-permute-done | bytes 196640 | tf_op jit(solution)/shard_map/ppermute | solution.py:217
  43.7 7.5 %collective-permute-start.3 = (bf16[256,384]{1,0:T(8,128)(2,1)S(1)}, bf16[256,384]{1,0:T(8,128)(2,1)S(1)}, u32[]{:S(2)}, u32[]{:S(2)}) collective-permute-start(bf16[256,384]{1,0:T(8,128)(2,1)S(1)} %collective-permute-done.2.qa_ref), channel_id=1, source_target_pairs={{0,8},{8,0},{1,9},{9,1},{2,10},{10,2},{3,11},{11,3},{4,12},{12,4},... | collective-permute-start | bytes 589832 | tf_op jit(solution)/shard_map/ppermute | solution.py:218
  51.2 1.0 copy-done.1
  52.9 5.5 %all-to-all-start.1 = ((bf16[8,2,16,384]{3,2,1,0:T(8,128)(2,1)}), bf16[8,2,16,384]{3,2,1,0:T(8,128)(2,1)S(1)}, u32[]{:S(2)}, u32[]{:S(2)}) async-start(bf16[8,2,16,384]{3,2,1,0:T(8,128)(2,1)} %pack_kv.1), calls=%async_computation.1 | async-start | bytes 393216 | tf_op jit(solution)/shard_map/all_to_all | solution.py:223
  58.5 2.2 %collective-permute-start = (bf16[256,384]{1,0:T(8,128)(2,1)S(1)}, bf16[256,384]{1,0:T(8,128)(2,1)}, u32[]{:S(2)}, u32[]{:S(2)}) collective-permute-start(bf16[256,384]{1,0:T(8,128)(2,1)S(1)} %bitcast.6), channel_id=1, source_target_pairs={{0,8},{8,0},{1,9},{9,1},{2,10},{10,2},{3,11},{11,3},{4,12},{12,4},... | collective-permute-start | bytes 589832 | tf_op jit(solution)/shard_map/ppermute | solution.py:216
  60.7 21.5 %all-gather.3.cloned.1.call-done = bf16[16,128,384]{2,1,0:T(8,128)(2,1)} async-done(((bf16[2,128,384]{2,1,0:T(8,128)(2,1)}), bf16[16,128,384]{2,1,0:T(8,128)(2,1)}) %all-gather.3.cloned.1.call-update) | async-done | bytes 1572880 | tf_op jit(solution)/shard_map/all_gather | solution.py:211
  82.2 1.4 copy-done.2
  83.6 4.7 %attend.3 = (bf16[400,256]{1,0:T(8,128)(2,1)S(1)}, bf16[400,256]{1,0:T(8,128)(2,1)S(1)}) custom-call(s32[3]{0:T(128)S(1)} %pad_add_fusion.pos_ref, bf16[256,384]{1,0:T(8,128)(2,1)S(1)} %collective-permute-done.2.qa_ref, bf16[256,384]{1,0:T(8,128)(2,1)S(1)} %collective-permute-done.3.qb_ref, bf16[8,2,128,384]{3,2,1,0:T(8,128)(2,1)S(1)} %bitcast.9), custom_call_target="tpu_custom_call" | custom-call | flops 805306368 | bytes 524288 | tf_op jit(solution)/shard_map/attend/pallas_call | solution.py:123
  88.3 4.3 %collective-permute-start.4 = (bf16[400,256]{1,0:T(8,128)(2,1)S(1)}, bf16[400,256]{1,0:T(8,128)(2,1)S(1)}, u32[]{:S(2)}, u32[]{:S(2)}) collective-permute-start(bf16[400,256]{1,0:T(8,128)(2,1)S(1)} %get-tuple-element.15), channel_id=1, source_target_pairs={{0,8},{8,0},{1,9},{9,1},{2,10},{10,2},{3,11},{11,3},{4,12},{12,4},... | collective-permute-start | bytes 614408 | tf_op jit(solution)/shard_map/ppermute | solution.py:228
  92.7 5.1 %attend.2 = (bf16[400,256]{1,0:T(8,128)(2,1)S(1)}, bf16[400,256]{1,0:T(8,128)(2,1)S(1)}) custom-call(s32[3]{0:T(128)S(1)} %pad_add_fusion.pos_ref, bf16[256,384]{1,0:T(8,128)(2,1)S(1)} %bitcast.7, bf16[256,384]{1,0:T(8,128)(2,1)} %collective-permute-done.qb_ref, bf16[8,2,128,384]{3,2,1,0:T(8,128)(2,1)S(1)} %bitcast.10), custom_call_target="tpu_custom_call" | custom-call | flops 805306368 | bytes 524288 | tf_op jit(solution)/shard_map/attend/pallas_call | solution.py:123
  97.7 1.9 %collective-permute-start.1 = (bf16[400,256]{1,0:T(8,128)(2,1)S(1)}, bf16[400,256]{1,0:T(8,128)(2,1)S(1)}, u32[]{:S(2)}, u32[]{:S(2)}) collective-permute-start(bf16[400,256]{1,0:T(8,128)(2,1)S(1)} %get-tuple-element.13), channel_id=1, source_target_pairs={{0,8},{8,0},{1,9},{9,1},{2,10},{10,2},{3,11},{11,3},{4,12},{12,4},... | collective-permute-start | bytes 614408 | tf_op jit(solution)/shard_map/ppermute | solution.py:226
  99.8 2.2 %collective-permute-start.5 = (bf16[400,256]{1,0:T(8,128)(2,1)S(1)}, bf16[400,256]{1,0:T(8,128)(2,1)S(1)}, u32[]{:S(2)}, u32[]{:S(2)}) collective-permute-start(bf16[400,256]{1,0:T(8,128)(2,1)S(1)} %merge_two.1), channel_id=1, source_target_pairs={{0,128},{128,0},{1,129},{129,1},{2,130},{130,2},{3,131},{131,3},{4... | collective-permute-start | bytes 614408 | tf_op jit(solution)/shard_map/ppermute | solution.py:230
  102.0 5.8 %collective-permute-done.5.c_ref = bf16[400,256]{1,0:T(8,128)(2,1)S(1)} collective-permute-done((bf16[400,256]{1,0:T(8,128)(2,1)S(1)}, bf16[400,256]{1,0:T(8,128)(2,1)S(1)}, u32[]{:S(2)}, u32[]{:S(2)}) %collective-permute-start.5) | collective-permute-done | bytes 204832 | tf_op jit(solution)/shard_map/ppermute | solution.py:230
  108.6 12.5 %collective-permute-start.6 = (bf16[400,128]{1,0:T(8,128)(2,1)S(1)}, bf16[400,128]{1,0:T(8,128)(2,1)S(1)}, u32[]{:S(2)}, u32[]{:S(2)}) collective-permute-start(bf16[400,128]{1,0:T(8,128)(2,1)S(1)} %get-tuple-element.17), channel_id=1, source_target_pairs={{0,16},{16,0},{1,17},{17,1},{2,18},{18,2},{3,19},{19,3},{4,20},{20... | collective-permute-start | bytes 307208 | tf_op jit(solution)/shard_map/ppermute | solution.py:247
  121.1 1.6 own.1
  123.5 2.0 %project.1 = (f32[64,3072]{1,0:T(8,128)S(1)}, bf16[64,3072]{1,0:T(8,128)(2,1)}) custom-call(s32[3]{0:T(128)S(1)} %pad_add_fusion.pos_ref, f32[392,128]{1,0:T(8,128)S(1)} %get-tuple-element.16.keep_ref, bf16[400,128]{1,0:T(8,128)(2,1)S(1)} %collective-permute-done.6.other_ref, f32[392,128]{1,0:T(8,128)S(1)} %get-tuple-element.18.own_ref, ...), custom_call_target="tpu_custom_call" | custom-call | bytes 524288 | tf_op jit(solution)/shard_map/project/pallas_call | solution.py:249
  125.5 2.8 %collective-permute-start.7 = (bf16[64,3072]{1,0:T(8,128)(2,1)}, bf16[64,3072]{1,0:T(8,128)(2,1)S(1)}, u32[]{:S(2)}, u32[]{:S(2)}) collective-permute-start(bf16[64,3072]{1,0:T(8,128)(2,1)} %get-tuple-element.20), channel_id=1, source_target_pairs={{0,1},{1,0},{2,3},{3,2},{4,5},{5,4},{6,7},{7,6},{8,9},{9,8},{10,11... | collective-permute-start | bytes 1179656 | tf_op jit(solution)/shard_map/ppermute | solution.py:259
  128.4 7.3 %collective-permute-done.7 = bf16[64,3072]{1,0:T(8,128)(2,1)S(1)} collective-permute-done((bf16[64,3072]{1,0:T(8,128)(2,1)}, bf16[64,3072]{1,0:T(8,128)(2,1)S(1)}, u32[]{:S(2)}, u32[]{:S(2)}) %collective-permute-start.7) | collective-permute-done | bytes 393248 | tf_op jit(solution)/shard_map/ppermute | solution.py:259
  135.7 6.3 %collective-permute-start.8 = (bf16[32,3072]{1,0:T(8,128)(2,1)S(1)}, bf16[32,3072]{1,0:T(8,128)(2,1)S(1)}, u32[]{:S(2)}, u32[]{:S(2)}) collective-permute-start(bf16[32,3072]{1,0:T(8,128)(2,1)S(1)} %dynamic-slice_convert_fusion), channel_id=1, source_target_pairs={{0,2},{1,3},{2,0},{3,1},{4,6},{5,7},{6,4},{7,5},{8,10},{9,11},{10,... | collective-permute-start | bytes 589832 | tf_op jit(solution)/shard_map/ppermute | solution.py:259
  142.1 5.1 %collective-permute-done.8 = bf16[32,3072]{1,0:T(8,128)(2,1)S(1)} collective-permute-done((bf16[32,3072]{1,0:T(8,128)(2,1)S(1)}, bf16[32,3072]{1,0:T(8,128)(2,1)S(1)}, u32[]{:S(2)}, u32[]{:S(2)}) %collective-permute-start.8) | collective-permute-done | bytes 196640 | tf_op jit(solution)/shard_map/ppermute | solution.py:259
  147.3 18.5 %collective-permute-start.9 = (bf16[16,3072]{1,0:T(8,128)(2,1)S(1)}, bf16[16,3072]{1,0:T(8,128)(2,1)S(1)}, u32[]{:S(2)}, u32[]{:S(2)}) collective-permute-start(bf16[16,3072]{1,0:T(8,128)(2,1)S(1)} %dynamic-slice_convert_fusion.1), channel_id=1, source_target_pairs={{0,4},{1,5},{2,6},{3,7},{4,0},{5,1},{6,2},{7,3},{8,12},{9,13},{10,... | collective-permute-start | bytes 294920 | tf_op jit(solution)/shard_map/ppermute | solution.py:259
  165.8 8.0 %collective-permute-done.9 = bf16[16,3072]{1,0:T(8,128)(2,1)S(1)} collective-permute-done((bf16[16,3072]{1,0:T(8,128)(2,1)S(1)}, bf16[16,3072]{1,0:T(8,128)(2,1)S(1)}, u32[]{:S(2)}, u32[]{:S(2)}) %collective-permute-start.9) | collective-permute-done | bytes 98336 | tf_op jit(solution)/shard_map/ppermute | solution.py:259
  (29 shorter events, 4.8 us)
Async XLA Ops:
  7.2 75.1 %all-gather.3.cloned.1.call-start = ((), (), s32[]{:S(2)}) async-start(), calls=%async_computation.2 | async-start | bytes 1769472 | tf_op jit(solution)/shard_map/all_gather | solution.py:211
  36.9 6.8 %collective-permute-start.2 = (bf16[256,384]{1,0:T(8,128)(2,1)S(1)}, bf16[256,384]{1,0:T(8,128)(2,1)S(1)}, u32[]{:S(2)}, u32[]{:S(2)}) collective-permute-start(bf16[256,384]{1,0:T(8,128)(2,1)S(1)} %bitcast.5), channel_id=1, source_target_pairs={{0,128},{128,0},{1,129},{129,1},{2,130},{130,2},{3,131},{131,3},{4... | collective-permute-start | bytes 589832 | tf_op jit(solution)/shard_map/ppermute | solution.py:217
  43.7 17.0 %collective-permute-start.3 = (bf16[256,384]{1,0:T(8,128)(2,1)S(1)}, bf16[256,384]{1,0:T(8,128)(2,1)S(1)}, u32[]{:S(2)}, u32[]{:S(2)}) collective-permute-start(bf16[256,384]{1,0:T(8,128)(2,1)S(1)} %collective-permute-done.2.qa_ref), channel_id=1, source_target_pairs={{0,8},{8,0},{1,9},{9,1},{2,10},{10,2},{3,11},{11,3},{4,12},{12,4},... | collective-permute-start | bytes 589832 | tf_op jit(solution)/shard_map/ppermute | solution.py:218
  51.2 1.0 copy-start.1
  52.9 68.2 %all-to-all-start.1 = ((bf16[8,2,16,384]{3,2,1,0:T(8,128)(2,1)}), bf16[8,2,16,384]{3,2,1,0:T(8,128)(2,1)S(1)}, u32[]{:S(2)}, u32[]{:S(2)}) async-start(bf16[8,2,16,384]{3,2,1,0:T(8,128)(2,1)} %pack_kv.1), calls=%async_computation.1 | async-start | bytes 393216 | tf_op jit(solution)/shard_map/all_to_all | solution.py:223
  58.5 34.2 %collective-permute-start = (bf16[256,384]{1,0:T(8,128)(2,1)S(1)}, bf16[256,384]{1,0:T(8,128)(2,1)}, u32[]{:S(2)}, u32[]{:S(2)}) collective-permute-start(bf16[256,384]{1,0:T(8,128)(2,1)S(1)} %bitcast.6), channel_id=1, source_target_pairs={{0,8},{8,0},{1,9},{9,1},{2,10},{10,2},{3,11},{11,3},{4,12},{12,4},... | collective-permute-start | bytes 589832 | tf_op jit(solution)/shard_map/ppermute | solution.py:216
  82.2 1.4 copy-start.2
  83.6 9.0 %copy-start.3 = (bf16[16,128,384]{2,1,0:T(8,128)(2,1)S(1)}, bf16[16,128,384]{2,1,0:T(8,128)(2,1)}, u32[]{:S(2)}) copy-start(bf16[16,128,384]{2,1,0:T(8,128)(2,1)} %all-gather.3.cloned.1.call-done) | copy-start | bytes 4718596
  88.3 35.1 %copy-start = (bf16[384,3072]{1,0:T(8,128)(2,1)S(1)}, bf16[384,3072]{1,0:T(8,128)(2,1)}, u32[]{:S(2)}) copy-start(bf16[384,3072]{1,0:T(8,128)(2,1)} %w_ref.1) | copy-start | bytes 7077892
  88.3 11.3 %collective-permute-start.4 = (bf16[400,256]{1,0:T(8,128)(2,1)S(1)}, bf16[400,256]{1,0:T(8,128)(2,1)S(1)}, u32[]{:S(2)}, u32[]{:S(2)}) collective-permute-start(bf16[400,256]{1,0:T(8,128)(2,1)S(1)} %get-tuple-element.15), channel_id=1, source_target_pairs={{0,8},{8,0},{1,9},{9,1},{2,10},{10,2},{3,11},{11,3},{4,12},{12,4},... | collective-permute-start | bytes 614408 | tf_op jit(solution)/shard_map/ppermute | solution.py:228
  97.7 4.3 %collective-permute-start.1 = (bf16[400,256]{1,0:T(8,128)(2,1)S(1)}, bf16[400,256]{1,0:T(8,128)(2,1)S(1)}, u32[]{:S(2)}, u32[]{:S(2)}) collective-permute-start(bf16[400,256]{1,0:T(8,128)(2,1)S(1)} %get-tuple-element.13), channel_id=1, source_target_pairs={{0,8},{8,0},{1,9},{9,1},{2,10},{10,2},{3,11},{11,3},{4,12},{12,4},... | collective-permute-start | bytes 614408 | tf_op jit(solution)/shard_map/ppermute | solution.py:226
  99.8 8.0 %collective-permute-start.5 = (bf16[400,256]{1,0:T(8,128)(2,1)S(1)}, bf16[400,256]{1,0:T(8,128)(2,1)S(1)}, u32[]{:S(2)}, u32[]{:S(2)}) collective-permute-start(bf16[400,256]{1,0:T(8,128)(2,1)S(1)} %merge_two.1), channel_id=1, source_target_pairs={{0,128},{128,0},{1,129},{129,1},{2,130},{130,2},{3,131},{131,3},{4... | collective-permute-start | bytes 614408 | tf_op jit(solution)/shard_map/ppermute | solution.py:230
  108.6 14.9 %collective-permute-start.6 = (bf16[400,128]{1,0:T(8,128)(2,1)S(1)}, bf16[400,128]{1,0:T(8,128)(2,1)S(1)}, u32[]{:S(2)}, u32[]{:S(2)}) collective-permute-start(bf16[400,128]{1,0:T(8,128)(2,1)S(1)} %get-tuple-element.17), channel_id=1, source_target_pairs={{0,16},{16,0},{1,17},{17,1},{2,18},{18,2},{3,19},{19,3},{4,20},{20... | collective-permute-start | bytes 307208 | tf_op jit(solution)/shard_map/ppermute | solution.py:247
  125.5 48.3 %copy-start.4 = (bf16[16,3072]{1,0:T(8,128)(2,1)S(1)}, bf16[16,3072]{1,0:T(8,128)(2,1)}, u32[]{:S(2)}) copy-start(bf16[16,3072]{1,0:T(8,128)(2,1)} %param.9) | copy-start | bytes 294916
  125.5 48.3 %copy-start.5 = (f32[3072]{0:T(1024)S(1)}, f32[3072]{0:T(1024)}, u32[]{:S(2)}) copy-start(f32[3072]{0:T(1024)} %param.8) | copy-start | bytes 36868
  125.5 10.1 %collective-permute-start.7 = (bf16[64,3072]{1,0:T(8,128)(2,1)}, bf16[64,3072]{1,0:T(8,128)(2,1)S(1)}, u32[]{:S(2)}, u32[]{:S(2)}) collective-permute-start(bf16[64,3072]{1,0:T(8,128)(2,1)} %get-tuple-element.20), channel_id=1, source_target_pairs={{0,1},{1,0},{2,3},{3,2},{4,5},{5,4},{6,7},{7,6},{8,9},{9,8},{10,11... | collective-permute-start | bytes 1179656 | tf_op jit(solution)/shard_map/ppermute | solution.py:259
  135.7 11.5 %collective-permute-start.8 = (bf16[32,3072]{1,0:T(8,128)(2,1)S(1)}, bf16[32,3072]{1,0:T(8,128)(2,1)S(1)}, u32[]{:S(2)}, u32[]{:S(2)}) collective-permute-start(bf16[32,3072]{1,0:T(8,128)(2,1)S(1)} %dynamic-slice_convert_fusion), channel_id=1, source_target_pairs={{0,2},{1,3},{2,0},{3,1},{4,6},{5,7},{6,4},{7,5},{8,10},{9,11},{10,... | collective-permute-start | bytes 589832 | tf_op jit(solution)/shard_map/ppermute | solution.py:259
  147.3 26.5 %collective-permute-start.9 = (bf16[16,3072]{1,0:T(8,128)(2,1)S(1)}, bf16[16,3072]{1,0:T(8,128)(2,1)S(1)}, u32[]{:S(2)}, u32[]{:S(2)}) collective-permute-start(bf16[16,3072]{1,0:T(8,128)(2,1)S(1)} %dynamic-slice_convert_fusion.1), channel_id=1, source_target_pairs={{0,4},{1,5},{2,6},{3,7},{4,0},{5,1},{6,2},{7,3},{8,12},{9,13},{10,... | collective-permute-start | bytes 294920 | tf_op jit(solution)/shard_map/ppermute | solution.py:259
Sparse Core Ops, SparseCore 0:
  11.2 70.9 all-gather.2

commit v2 on v1

v2 whole, which is shorter than its diff:
```python
import functools
import math

import jax
import jax.numpy as jnp
from jax import lax
from jax.experimental import pallas as pl
from jax.experimental.pallas import tpu as pltpu
from jax.sharding import Mesh, PartitionSpec as P

HEAD_DIM = 128
AXES = ("y", "x", "zh", "core", "head")
SLAB_AXES = AXES[:-1]
SIZES = (4, 4, 2, 2, 8)
N_HEAD = 8
HEADS_HERE = 3
WIDTH = HEADS_HERE * HEAD_DIM
SLAB = 128
PIECE = SLAB // N_HEAD
D = N_HEAD * WIDTH
KEY_SLABS = 8
KEYS = KEY_SLABS * SLAB
PAIR = 2 * SLAB
QUERY_SLABS = 4
QUERY_FROM = (0, 1, 3, 2)
PARTS = 2
LONG = 40_000_000_000
STAT_ROWS = 16
ROWS = WIDTH + STAT_ROWS
LOG2E = 1.4426950408889634
FACTOR = LOG2E / math.sqrt(HEAD_DIM)
PIECE_ORDER = (0, 4, 2, 6, 1, 5, 3, 7)

VMEM = pl.BlockSpec(memory_space=pltpu.VMEM)
SMEM = pl.BlockSpec(memory_space=pltpu.SMEM)
ANY = pl.BlockSpec(memory_space=pl.ANY)
HBM = pl.BlockSpec(memory_space=pltpu.HBM)
BF16 = jnp.bfloat16
F32 = jnp.float32


def swap(n, bit):
    return [(i, i ^ bit) for i in range(n)]


def shift(n, by):
    return [(i, (i + by) % n) for i in range(n)]


def call(body, out_shape, n_in, scratch=(), in_specs=None, flops=0, vmem=None, name=None):
    out_specs = jax.tree.map(lambda _: VMEM, out_shape)
    return pl.pallas_call(
        body,
        out_shape=out_shape,
        in_specs=in_specs or [VMEM] * n_in,
        out_specs=out_specs,
        scratch_shapes=list(scratch),
        compiler_params=pltpu.CompilerParams(vmem_limit_bytes=vmem or (8 << 20)),
        cost_estimate=pl.CostEstimate(flops=flops, bytes_accessed=1 << 19, transcendentals=0),
        name=name,
    )


def shape(dims, dtype):
    return jax.ShapeDtypeStruct(dims, dtype)


def pack_body(fresh_ref, out_ref):
    for h in range(N_HEAD):
        for part in range(3):
            out_ref[h, part] = fresh_ref[part, :, h * WIDTH : (h + 1) * WIDTH]


def unpack_body(n_after, pieces_ref, *rest):
    q_ref, next_ref = rest[n_after:]
    for piece in range(N_HEAD):
        rows = slice(piece * PIECE, (piece + 1) * PIECE)
        q_ref[rows] = pieces_ref[piece, 0]
        for part in range(2):
            next_ref[part, rows] = pieces_ref[piece, 1 + part]


def join_body(*refs):
    for i in range(QUERY_SLABS):
        refs[-1][i * SLAB : (i + 1) * SLAB] = refs[i][...]


def after_body(block_ref, *rest):
    rest[-1][...] = block_ref[...]


def stat_rows(lses):
    n = lses[0].shape[1]
    high = [v.astype(BF16).astype(F32) for v in lses]
    rest = [v - w for v, w in zip(lses, high)]
    mid = [v.astype(BF16).astype(F32) for v in rest]
    low = [v - w for v, w in zip(rest, mid)]
    pad = jnp.zeros((STAT_ROWS - 3 * HEADS_HERE, n), F32)
    return jnp.concatenate(high + mid + low + [pad], axis=0).astype(BF16)


def read_stats(rows):
    rows = rows.astype(F32)
    n = HEADS_HERE
    return [rows[h : h + 1] + rows[n + h : n + h + 1] + rows[2 * n + h : 2 * n + h + 1] for h in range(n)]


def scores_of(keys, queries):
    return lax.dot_general(keys, queries, (((1,), (1,)), ((), ())), preferred_element_type=F32)


def attend_body(q_core_ref, q_own_ref, next_ref, *rest):
    old_refs, (core_ref, own_ref, s_ref) = rest[:KEY_SLABS], rest[KEY_SLABS:]
    blocks = [
        (q_ref, out_ref, slice(i * PAIR, (i + 1) * PAIR), q_ref is q_own_ref and i == 0)
        for q_ref, out_ref in ((q_core_ref, core_ref), (q_own_ref, own_ref))
        for i in range(QUERY_SLABS // 2)
    ]
    lses = [[] for _ in blocks]
    for h in range(HEADS_HERE):
        cols = slice(h * HEAD_DIM, (h + 1) * HEAD_DIM)
        keys, values = (jnp.concatenate([r[part, :, cols] for r in old_refs], 0) for part in range(2))
        values_t = values.T
        for i, (q_ref, out_ref, queries, with_own) in enumerate(blocks):
            s_ref[i % 2] = scores_of(keys, q_ref[queries, cols])
            if with_own:
                s_ref[i % 2, :SLAB, :SLAB] = scores_of(next_ref[0, :, cols], q_ref[:SLAB, cols])
            s = s_ref[i % 2]
            top = jnp.max(s, axis=0, keepdims=True)
            weights = jnp.exp2((s - top) * FACTOR)
            total = jnp.sum(weights, axis=0, keepdims=True)
            weights = weights.astype(BF16)
            if with_own:
                fresh = jnp.dot(next_ref[1, :, cols].T, weights[:SLAB, :SLAB], preferred_element_type=F32)
                later = jnp.dot(values_t[:, SLAB:], weights[SLAB:], preferred_element_type=F32)
                first = jnp.dot(values_t[:, :SLAB], weights[:SLAB, SLAB:], preferred_element_type=F32)
                summed = later + jnp.concatenate([fresh, first], axis=1)
            else:
                summed = jnp.dot(values_t, weights, preferred_element_type=F32)
            out_ref[h * HEAD_DIM : (h + 1) * HEAD_DIM, queries] = (summed / total).astype(BF16)
            lses[i].append(top * FACTOR + jnp.log2(total))
    for (_, out_ref, queries, _), found in zip(blocks, lses):
        out_ref[WIDTH:, queries] = stat_rows(found)


def attend(q_core, q_own, next_kv, *keys_values):
    return call(
        attend_body,
        (shape((ROWS, QUERY_SLABS * SLAB), BF16),) * 2,
        3 + KEY_SLABS,
        scratch=[pltpu.VMEM((2, KEYS, PAIR), F32)],
        vmem=20 << 20,
        flops=8 * HEADS_HERE * KEYS * QUERY_SLABS * SLAB * HEAD_DIM,
        name="attend",
    )(q_core, q_own, next_kv, *keys_values)


def merge(outs, lses):
    top = functools.reduce(jnp.maximum, lses)
    shares = [jnp.exp2(v - top) for v in lses]
    total = sum(shares)
    merged = sum(o.astype(F32) * (w / total) for o, w in zip(outs, shares))
    return merged, top + jnp.log2(total)


def merge_core_body(y_ref, a_ref, b_ref, out_ref):
    for i, by in enumerate(QUERY_FROM):
        cols = pl.ds(i * SLAB, SLAB)
        parts = (a_ref.at[:, cols], b_ref.at[:, cols])
        stats = [read_stats(p[WIDTH:]) for p in parts]
        place = lax.rem(y_ref[0] + QUERY_SLABS - by, QUERY_SLABS)
        lses = []
        for h in range(HEADS_HERE):
            rows = slice(h * HEAD_DIM, (h + 1) * HEAD_DIM)
            out, lse = merge([p[rows] for p in parts], [v[h] for v in stats])
            out_ref[place, rows] = out.astype(BF16)
            lses.append(lse)
        out_ref[place, WIDTH:] = stat_rows(lses)


def project_body(pos_ref, parts_ref, w_hbm, *rest):
    *outs, att_ref, proj_ref, w_ref, sem = rest
    copy = pltpu.make_async_copy(w_hbm, w_ref, sem)
    copy.start()
    stats = [read_stats(parts_ref[y, WIDTH:]) for y in range(QUERY_SLABS)]
    for h in range(HEADS_HERE):
        rows = slice(h * HEAD_DIM, (h + 1) * HEAD_DIM)
        out, _ = merge([parts_ref[y, rows] for y in range(QUERY_SLABS)], [v[h] for v in stats])
        att_ref[:, rows] = out.T.astype(BF16)
    copy.wait()
    proj = jnp.dot(att_ref[...], w_ref[...], preferred_element_type=F32)
    for at, piece in enumerate(PIECE_ORDER):
        proj_ref[at * PIECE : (at + 1) * PIECE] = proj[piece * PIECE : (piece + 1) * PIECE]
    half = SLAB // 2
    bit = pos_ref[0]
    mine = pl.ds(pl.multiple_of(bit * half, half), half)
    theirs = pl.ds(pl.multiple_of((1 - bit) * half, half), half)
    for part, (keep_out, send_out) in enumerate(zip(outs[0::2], outs[1::2])):
        cols = slice(part * D // PARTS, (part + 1) * D // PARTS)
        keep_out[...] = proj_ref[mine, cols]
        send_out[...] = proj_ref[theirs, cols].astype(BF16)


def local(fresh_qkv, stale_kv, out_weight, branch_gate, residual):
    head = lax.axis_index("head")
    pos = jnp.stack([head % 2]).astype(jnp.int32)
    y = jnp.stack([lax.axis_index("y")]).astype(jnp.int32)

    packed = call(pack_body, shape((N_HEAD, 3, PIECE, WIDTH), BF16), 1, name="pack")(fresh_qkv)
    pieces = lax.all_to_all(packed, "head", 0, 0, tiled=True)

    other_z = lax.ppermute(stale_kv, "zh", swap(2, 1))
    other_z = call(after_body, shape(other_z.shape, BF16), 1, flops=LONG, name="after")(other_z)
    here = [stale_kv] + [lax.ppermute(stale_kv, "x", shift(4, by)) for by in (1, 3, 2)]

    q_own, next_kv = call(
        functools.partial(unpack_body, 2),
        (shape((SLAB, WIDTH), BF16), shape((2, SLAB, WIDTH), BF16)),
        3,
        in_specs=[VMEM] + [ANY] * 2,
        name="unpack",
    )(pieces, *here[1:3])
    q_slabs = [q_own] + [lax.ppermute(q_own, "y", shift(4, by)) for by in QUERY_FROM[1:]]

    q_all = call(join_body, shape((QUERY_SLABS * SLAB, WIDTH), BF16), 4, name="join")(*q_slabs)

    q_core = lax.ppermute(q_all, "core", swap(2, 1))
    there = [other_z] + [lax.ppermute(other_z, "x", shift(4, by)) for by in (1, 3, 2)]

    m_there, m_own = attend(q_core, q_all, next_kv, *here, *there)
    m_core = lax.ppermute(m_there, "core", swap(2, 1))
    merged = call(
        merge_core_body,
        shape((QUERY_SLABS, ROWS, SLAB), BF16),
        3,
        in_specs=[SMEM, VMEM, VMEM],
        name="merge_core",
    )(y, m_own, m_core)
    by_y = lax.all_to_all(merged, "y", 0, 0, tiled=True)

    half = (SLAB // 2, D // PARTS)
    parts = call(
        project_body,
        (shape(half, F32), shape(half, BF16)) * PARTS,
        3,
        scratch=[
            pltpu.VMEM((SLAB, WIDTH), BF16),
            pltpu.VMEM((SLAB, D), F32),
            pltpu.VMEM((WIDTH, D), BF16),
            pltpu.SemaphoreType.DMA,
        ],
        in_specs=[SMEM, VMEM, HBM],
        vmem=12 << 20,
        name="project",
    )(pos, by_y, out_weight)

    def halve(kept, bit):
        rows = kept.shape[0] // 2
        mine = (head // bit) % 2
        sent = lax.dynamic_slice_in_dim(kept, (1 - mine) * rows, rows, 0).astype(BF16)
        return lax.dynamic_slice_in_dim(kept, mine * rows, rows, 0), sent

    def add(kept, sent, bit):
        return kept + lax.ppermute(sent, "head", swap(N_HEAD, bit)).astype(F32)

    sums = []
    for kept, sent in zip(parts[0::2], parts[1::2]):
        kept, sent = halve(add(kept, sent, 1), 2)
        sums.append(halve(add(kept, sent, 2), 4))
    kept, sent = (jnp.concatenate(side, axis=1) for side in zip(*sums))
    projected = add(kept, sent, 4)
    block_out = (residual.astype(F32) + branch_gate[None, :] * projected).astype(BF16)
    return block_out, next_kv


def solution(mesh):
    fine = Mesh(mesh.devices.reshape(SIZES), AXES)
    return jax.shard_map(
        local,
        mesh=fine,
        in_specs=(
            P(None, AXES, None),
            P(None, SLAB_AXES, "head"),
            P("head", None),
            P(),
            P(AXES, None),
        ),
        out_specs=(P(AXES, None), P(None, SLAB_AXES, "head")),
        check_vma=False,
    )
```

time: 182 us -> 134 us (0.74)
  blocking collectives: 28.1 us -> 0 us
  waiting for transfers between devices: 52.7 us -> 36 us
  starting transfers between devices: 67 us -> 82 us
  between operations: 14.3 us -> 1.09 us
  Pallas kernels: 15 us -> 12 us
    all_to_all x1 -> x0, blocking collectives: 28.1 us -> none  [local(): q_all = lax.all_to_all(q_packed, ('zh', 'head'), 0, 0, tiled=True)]
    all_gather x1 -> x0, waiting for transfers between devices: 21.5 us -> none  [local(): kv = lax.all_gather(stale_kv, KEY_AXES, axis=0, tiled=False)]
    all_to_all x1 -> x2, starting transfers between devices: 5.52 us -> 16.5 us  [the longest x1 13.1 us: local(): pieces = lax.all_to_all(packed, 'head', 0, 0, tiled=True)]
    all_to_all x1 -> x2, waiting for transfers between devices: 0.01 us -> 8.58 us  [the longest x1 7.95 us: local(): by_y = lax.all_to_all(merged, 'y', 0, 0, tiled=True)]
    ppermute x10 -> x17, starting transfers between devices: 61.5 us -> 65.5 us  [the longest x5 16.2 us: add(): return kept + lax.ppermute(sent, 'head', swap(N_HEAD, bit)).astype(F32)]
    ppermute x10 -> x17, waiting for transfers between devices: 30.5 us -> 27.4 us  [the longest x5 19.4 us: add(): return kept + lax.ppermute(sent, 'head', swap(N_HEAD, bit)).astype(F32)]
    pallas_call x8 -> x7, Pallas kernels: 15 us -> 12 us  [the longest x1 7.82 us: attend(): call(attend_body, (shape((ROWS, QUERY_SLABS * SLAB), BF16),) * 2, 3 + KEY...]
  transfers between devices with their start and end apart: 12 -> 19, of which waited for: 7 -> 10; matrix products, arithmetic and copies ran while one was open for 1% -> 0% of each run, Pallas kernels for 7% -> 1%
where the time goes in v2:
time: 134 us
  starting transfers between devices  82 us (61%)
  waiting for transfers between devices  36 us (27%)
  Pallas kernels  12 us (9%)
  local copies, waits for them, and re-layouts  1.76 us (1%)
    ppermute x5, waiting for transfers between devices, add(): return kept + lax.ppermute(sent, 'head', swap(N_HEAD, bit)).astype(F32)  19.4 us
    ppermute x5, starting transfers between devices, add(): return kept + lax.ppermute(sent, 'head', swap(N_HEAD, bit)).astype(F32)  16.2 us
    all_to_all x1, starting transfers between devices, local(): pieces = lax.all_to_all(packed, 'head', 0, 0, tiled=True)  13.1 us
    ppermute x3, starting transfers between devices, local(): lax.ppermute(stale_kv, 'x', shift(4, by))  11 us
    ppermute x3, starting transfers between devices, local(): lax.ppermute(q_own, 'y', shift(4, by))  10.1 us
    ppermute x3, starting transfers between devices, local(): lax.ppermute(other_z, 'x', shift(4, by))  9.79 us
    all_to_all x1, waiting for transfers between devices, local(): by_y = lax.all_to_all(merged, 'y', 0, 0, tiled=True)  7.95 us
    ppermute x1, starting transfers between devices, local(): other_z = lax.ppermute(stale_kv, 'zh', swap(2, 1))  7.94 us
  transfers between devices with their start and end apart: 19, of which 10 were waited for; matrix products, arithmetic and copies ran while one was open for 0% of the time, Pallas kernels for 1%

profile of v2, /device:TPU:1, one launch (start us, length us, event | category | flops | bytes accessed | tf_op | source)
XLA Modules:
  0.0 133.7 jit_solution(755806512220320408)
XLA Ops:
  2.3 13.1 %all-to-all-start = ((bf16[8,3,16,384]{3,2,1,0:T(8,128)(2,1)}), bf16[8,3,16,384]{3,2,1,0:T(8,128)(2,1)S(1)}, u32[]{:S(2)}, u32[]{:S(2)}) async-start(bf16[8,3,16,384]{3,2,1,0:T(8,128)(2,1)} %pack.1), calls=%async_computation | async-start | bytes 589824 | tf_op jit(solution)/shard_map/all_to_all | solution.py:210
  15.4 4.4 %collective-permute-start.1 = (bf16[2,128,384]{2,1,0:T(8,128)(2,1)}, bf16[2,128,384]{2,1,0:T(8,128)(2,1)S(1)}, u32[]{:S(2)}, u32[]{:S(2)}) collective-permute-start(bf16[2,128,384]{2,1,0:T(8,128)(2,1)} %rest_0_.1), channel_id=1, source_target_pairs={{0,96},{32,0},{64,32},{96,64},{1,97},{33,1},{65,33},{97,65},{2,98}... | collective-permute-start | bytes 589832 | tf_op jit(solution)/shard_map/ppermute | solution.py:214
  21.7 7.9 %collective-permute-start.7 = (bf16[2,128,384]{2,1,0:T(8,128)(2,1)}, bf16[2,128,384]{2,1,0:T(8,128)(2,1)S(1)}, u32[]{:S(2)}, u32[]{:S(2)}) collective-permute-start(bf16[2,128,384]{2,1,0:T(8,128)(2,1)} %rest_0_.1), channel_id=1, source_target_pairs={{0,16},{16,0},{1,17},{17,1},{2,18},{18,2},{3,19},{19,3},{4,20},{20... | collective-permute-start | bytes 589832 | tf_op jit(solution)/shard_map/ppermute | solution.py:212
  31.0 4.8 %collective-permute-start.4 = (bf16[128,384]{1,0:T(8,128)(2,1)S(1)}, bf16[128,384]{1,0:T(8,128)(2,1)S(1)}, u32[]{:S(2)}, u32[]{:S(2)}) collective-permute-start(bf16[128,384]{1,0:T(8,128)(2,1)S(1)} %get-tuple-element.10.refs_0_), channel_id=1, source_target_pairs={{0,256},{128,384},{256,0},{384,128},{1,257},{129,385},{257,1},{385... | collective-permute-start | bytes 294920 | tf_op jit(solution)/shard_map/ppermute | solution.py:223
  35.8 2.7 %collective-permute-start.3 = (bf16[128,384]{1,0:T(8,128)(2,1)S(1)}, bf16[128,384]{1,0:T(8,128)(2,1)S(1)}, u32[]{:S(2)}, u32[]{:S(2)}) collective-permute-start(bf16[128,384]{1,0:T(8,128)(2,1)S(1)} %get-tuple-element.10.refs_0_), channel_id=1, source_target_pairs={{0,384},{128,0},{256,128},{384,256},{1,385},{129,1},{257,129},{385... | collective-permute-start | bytes 294920 | tf_op jit(solution)/shard_map/ppermute | solution.py:223
  38.5 2.6 %collective-permute-start.2 = (bf16[128,384]{1,0:T(8,128)(2,1)S(1)}, bf16[128,384]{1,0:T(8,128)(2,1)S(1)}, u32[]{:S(2)}, u32[]{:S(2)}) collective-permute-start(bf16[128,384]{1,0:T(8,128)(2,1)S(1)} %get-tuple-element.10.refs_0_), channel_id=1, source_target_pairs={{0,128},{128,256},{256,384},{384,0},{1,129},{129,257},{257,385},{3... | collective-permute-start | bytes 294920 | tf_op jit(solution)/shard_map/ppermute | solution.py:223
  41.1 4.7 %collective-permute-start.6 = (bf16[2,128,384]{2,1,0:T(8,128)(2,1)}, bf16[2,128,384]{2,1,0:T(8,128)(2,1)S(1)}, u32[]{:S(2)}, u32[]{:S(2)}) collective-permute-start(bf16[2,128,384]{2,1,0:T(8,128)(2,1)} %rest_0_.1), channel_id=1, source_target_pairs={{0,64},{32,96},{64,0},{96,32},{1,65},{33,97},{65,1},{97,33},{2,66}... | collective-permute-start | bytes 589832 | tf_op jit(solution)/shard_map/ppermute | solution.py:214
  45.9 7.2 %collective-permute-start.5 = (bf16[512,384]{1,0:T(8,128)(2,1)S(1)}, bf16[512,384]{1,0:T(8,128)(2,1)S(1)}, u32[]{:S(2)}, u32[]{:S(2)}) collective-permute-start(bf16[512,384]{1,0:T(8,128)(2,1)S(1)} %join.1.q_own_ref), channel_id=1, source_target_pairs={{0,8},{8,0},{1,9},{9,1},{2,10},{10,2},{3,11},{11,3},{4,12},{12,4},... | collective-permute-start | bytes 1179656 | tf_op jit(solution)/shard_map/ppermute | solution.py:227
  53.1 4.5 %collective-permute-start.10 = (bf16[2,128,384]{2,1,0:T(8,128)(2,1)S(1)}, bf16[2,128,384]{2,1,0:T(8,128)(2,1)S(1)}, u32[]{:S(2)}, u32[]{:S(2)}) collective-permute-start(bf16[2,128,384]{2,1,0:T(8,128)(2,1)S(1)} %after.1.rest_4_), channel_id=1, source_target_pairs={{0,64},{32,96},{64,0},{96,32},{1,65},{33,97},{65,1},{97,33},{2,66}... | collective-permute-start | bytes 589832 | tf_op jit(solution)/shard_map/ppermute | solution.py:228
  57.6 2.8 %collective-permute-start.9 = (bf16[2,128,384]{2,1,0:T(8,128)(2,1)S(1)}, bf16[2,128,384]{2,1,0:T(8,128)(2,1)S(1)}, u32[]{:S(2)}, u32[]{:S(2)}) collective-permute-start(bf16[2,128,384]{2,1,0:T(8,128)(2,1)S(1)} %after.1.rest_4_), channel_id=1, source_target_pairs={{0,96},{32,0},{64,32},{96,64},{1,97},{33,1},{65,33},{97,65},{2,98}... | collective-permute-start | bytes 589832 | tf_op jit(solution)/shard_map/ppermute | solution.py:228
  60.4 2.5 %collective-permute-start.8 = (bf16[2,128,384]{2,1,0:T(8,128)(2,1)S(1)}, bf16[2,128,384]{2,1,0:T(8,128)(2,1)S(1)}, u32[]{:S(2)}, u32[]{:S(2)}) collective-permute-start(bf16[2,128,384]{2,1,0:T(8,128)(2,1)S(1)} %after.1.rest_4_), channel_id=1, source_target_pairs={{0,32},{32,64},{64,96},{96,0},{1,33},{33,65},{65,97},{97,1},{2,34}... | collective-permute-start | bytes 589832 | tf_op jit(solution)/shard_map/ppermute | solution.py:228
  63.0 4.1 %collective-permute-done.9.rest_6_ = bf16[2,128,384]{2,1,0:T(8,128)(2,1)S(1)} collective-permute-done((bf16[2,128,384]{2,1,0:T(8,128)(2,1)S(1)}, bf16[2,128,384]{2,1,0:T(8,128)(2,1)S(1)}, u32[]{:S(2)}, u32[]{:S(2)}) %collective-permute-start.9) | collective-permute-done | bytes 196640 | tf_op jit(solution)/shard_map/ppermute | solution.py:228
  67.2 2.2 %collective-permute-done.8.rest_5_ = bf16[2,128,384]{2,1,0:T(8,128)(2,1)S(1)} collective-permute-done((bf16[2,128,384]{2,1,0:T(8,128)(2,1)S(1)}, bf16[2,128,384]{2,1,0:T(8,128)(2,1)S(1)}, u32[]{:S(2)}, u32[]{:S(2)}) %collective-permute-start.8) | collective-permute-done | bytes 196640 | tf_op jit(solution)/shard_map/ppermute | solution.py:228
  69.4 7.8 %attend.1 = (bf16[400,512]{1,0:T(8,128)(2,1)}, bf16[400,512]{1,0:T(8,128)(2,1)S(1)}) custom-call(bf16[512,384]{1,0:T(8,128)(2,1)S(1)} %collective-permute-done.5.q_core_ref, bf16[512,384]{1,0:T(8,128)(2,1)S(1)} %join.1.q_own_ref, bf16[2,128,384]{2,1,0:T(8,128)(2,1)S(1)} %copy-done.3, bf16[2,128,384]{2,1,0:T(8,128)(2,1)S(1)} %copy-done.2, ...), custom_call_target="tpu_custom_call" | custom-call | flops 1610612736 | bytes 524288 | tf_op jit(solution)/shard_map/attend/pallas_call | solution.py:147
  77.3 3.3 %collective-permute-start.11 = (bf16[400,512]{1,0:T(8,128)(2,1)}, bf16[400,512]{1,0:T(8,128)(2,1)S(1)}, u32[]{:S(2)}, u32[]{:S(2)}) collective-permute-start(bf16[400,512]{1,0:T(8,128)(2,1)} %get-tuple-element.13), channel_id=1, source_target_pairs={{0,8},{8,0},{1,9},{9,1},{2,10},{10,2},{3,11},{11,3},{4,12},{12,4},... | collective-permute-start | bytes 1228808 | tf_op jit(solution)/shard_map/ppermute | solution.py:231
  83.2 3.5 %all-to-all-start.1 = ((bf16[4,400,128]{2,1,0:T(8,128)(2,1)}), bf16[4,400,128]{2,1,0:T(8,128)(2,1)S(1)}, u32[]{:S(2)}, u32[]{:S(2)}) async-start(bf16[4,400,128]{2,1,0:T(8,128)(2,1)} %merge_core.1), calls=%async_computation.1 | async-start | bytes 819200 | tf_op jit(solution)/shard_map/all_to_all | solution.py:239
  86.6 8.0 %all-to-all-done.1.parts_ref = bf16[4,400,128]{2,1,0:T(8,128)(2,1)S(1)} async-done(((bf16[4,400,128]{2,1,0:T(8,128)(2,1)}), bf16[4,400,128]{2,1,0:T(8,128)(2,1)S(1)}, u32[]{:S(2)}, u32[]{:S(2)}) %all-to-all-start.1) | async-done | bytes 409632 | tf_op jit(solution)/shard_map/all_to_all | solution.py:239
  97.0 3.4 %collective-permute-start.12 = (bf16[64,1536]{1,0:T(8,128)(2,1)}, bf16[64,1536]{1,0:T(8,128)(2,1)S(1)}, u32[]{:S(2)}, u32[]{:S(2)}) collective-permute-start(bf16[64,1536]{1,0:T(8,128)(2,1)} %get-tuple-element.15), channel_id=1, source_target_pairs={{0,1},{1,0},{2,3},{3,2},{4,5},{5,4},{6,7},{7,6},{8,9},{9,8},{10,11... | collective-permute-start | bytes 589832 | tf_op jit(solution)/shard_map/ppermute | solution.py:264
  100.4 2.0 %collective-permute-start.14 = (bf16[64,1536]{1,0:T(8,128)(2,1)}, bf16[64,1536]{1,0:T(8,128)(2,1)S(1)}, u32[]{:S(2)}, u32[]{:S(2)}) collective-permute-start(bf16[64,1536]{1,0:T(8,128)(2,1)} %copy-done.4), channel_id=1, source_target_pairs={{0,1},{1,0},{2,3},{3,2},{4,5},{5,4},{6,7},{7,6},{8,9},{9,8},{10,11... | collective-permute-start | bytes 589832 | tf_op jit(solution)/shard_map/ppermute | solution.py:264
  104.5 2.9 %collective-permute-start.13 = (bf16[32,1536]{1,0:T(8,128)(2,1)S(1)}, bf16[32,1536]{1,0:T(8,128)(2,1)S(1)}, u32[]{:S(2)}, u32[]{:S(2)}) collective-permute-start(bf16[32,1536]{1,0:T(8,128)(2,1)S(1)} %dynamic-slice_convert_fusion.1), channel_id=1, source_target_pairs={{0,2},{1,3},{2,0},{3,1},{4,6},{5,7},{6,4},{7,5},{8,10},{9,11},{10,... | collective-permute-start | bytes 294920 | tf_op jit(solution)/shard_map/ppermute | solution.py:264
  109.2 2.6 %collective-permute-start.15 = (bf16[32,1536]{1,0:T(8,128)(2,1)S(1)}, bf16[32,1536]{1,0:T(8,128)(2,1)S(1)}, u32[]{:S(2)}, u32[]{:S(2)}) collective-permute-start(bf16[32,1536]{1,0:T(8,128)(2,1)S(1)} %dynamic-slice_convert_fusion), channel_id=1, source_target_pairs={{0,2},{1,3},{2,0},{3,1},{4,6},{5,7},{6,4},{7,5},{8,10},{9,11},{10,... | collective-permute-start | bytes 294920 | tf_op jit(solution)/shard_map/ppermute | solution.py:264
  112.0 6.0 %collective-permute-done.15 = bf16[32,1536]{1,0:T(8,128)(2,1)S(1)} collective-permute-done((bf16[32,1536]{1,0:T(8,128)(2,1)S(1)}, bf16[32,1536]{1,0:T(8,128)(2,1)S(1)}, u32[]{:S(2)}, u32[]{:S(2)}) %collective-permute-start.15) | collective-permute-done | bytes 98336 | tf_op jit(solution)/shard_map/ppermute | solution.py:264
  118.0 5.3 %collective-permute-start.16 = (bf16[16,3072]{1,0:T(8,128)(2,1)S(1)}, bf16[16,3072]{1,0:T(8,128)(2,1)S(1)}, u32[]{:S(2)}, u32[]{:S(2)}) collective-permute-start(bf16[16,3072]{1,0:T(8,128)(2,1)S(1)} %pad_maximum_fusion), channel_id=1, source_target_pairs={{0,4},{1,5},{2,6},{3,7},{4,0},{5,1},{6,2},{7,3},{8,12},{9,13},{10,... | collective-permute-start | bytes 294920 | tf_op jit(solution)/shard_map/ppermute | solution.py:264
  123.3 9.7 %collective-permute-done.16 = bf16[16,3072]{1,0:T(8,128)(2,1)S(1)} collective-permute-done((bf16[16,3072]{1,0:T(8,128)(2,1)S(1)}, bf16[16,3072]{1,0:T(8,128)(2,1)S(1)}, u32[]{:S(2)}, u32[]{:S(2)}) %collective-permute-start.16) | collective-permute-done | bytes 98336 | tf_op jit(solution)/shard_map/ppermute | solution.py:264
  (47 shorter events, 14.7 us)
Async XLA Ops:
  2.3 28.0 %all-to-all-start = ((bf16[8,3,16,384]{3,2,1,0:T(8,128)(2,1)}), bf16[8,3,16,384]{3,2,1,0:T(8,128)(2,1)S(1)}, u32[]{:S(2)}, u32[]{:S(2)}) async-start(bf16[8,3,16,384]{3,2,1,0:T(8,128)(2,1)} %pack.1), calls=%async_computation | async-start | bytes 589824 | tf_op jit(solution)/shard_map/all_to_all | solution.py:210
  15.4 14.3 %collective-permute-start.1 = (bf16[2,128,384]{2,1,0:T(8,128)(2,1)}, bf16[2,128,384]{2,1,0:T(8,128)(2,1)S(1)}, u32[]{:S(2)}, u32[]{:S(2)}) collective-permute-start(bf16[2,128,384]{2,1,0:T(8,128)(2,1)} %rest_0_.1), channel_id=1, source_target_pairs={{0,96},{32,0},{64,32},{96,64},{1,97},{33,1},{65,33},{97,65},{2,98}... | collective-permute-start | bytes 589832 | tf_op jit(solution)/shard_map/ppermute | solution.py:214
  19.8 9.9 %collective-permute-start = (bf16[2,128,384]{2,1,0:T(8,128)(2,1)}, bf16[2,128,384]{2,1,0:T(8,128)(2,1)S(1)}, u32[]{:S(2)}, u32[]{:S(2)}) collective-permute-start(bf16[2,128,384]{2,1,0:T(8,128)(2,1)} %rest_0_.1), channel_id=1, source_target_pairs={{0,32},{32,64},{64,96},{96,0},{1,33},{33,65},{65,97},{97,1},{2,34}... | collective-permute-start | bytes 589832 | tf_op jit(solution)/shard_map/ppermute | solution.py:214
  21.7 31.4 %collective-permute-start.7 = (bf16[2,128,384]{2,1,0:T(8,128)(2,1)}, bf16[2,128,384]{2,1,0:T(8,128)(2,1)S(1)}, u32[]{:S(2)}, u32[]{:S(2)}) collective-permute-start(bf16[2,128,384]{2,1,0:T(8,128)(2,1)} %rest_0_.1), channel_id=1, source_target_pairs={{0,16},{16,0},{1,17},{17,1},{2,18},{18,2},{3,19},{19,3},{4,20},{20... | collective-permute-start | bytes 589832 | tf_op jit(solution)/shard_map/ppermute | solution.py:212
  31.0 14.8 %collective-permute-start.4 = (bf16[128,384]{1,0:T(8,128)(2,1)S(1)}, bf16[128,384]{1,0:T(8,128)(2,1)S(1)}, u32[]{:S(2)}, u32[]{:S(2)}) collective-permute-start(bf16[128,384]{1,0:T(8,128)(2,1)S(1)} %get-tuple-element.10.refs_0_), channel_id=1, source_target_pairs={{0,256},{128,384},{256,0},{384,128},{1,257},{129,385},{257,1},{385... | collective-permute-start | bytes 294920 | tf_op jit(solution)/shard_map/ppermute | solution.py:223
  35.8 10.0 %collective-permute-start.3 = (bf16[128,384]{1,0:T(8,128)(2,1)S(1)}, bf16[128,384]{1,0:T(8,128)(2,1)S(1)}, u32[]{:S(2)}, u32[]{:S(2)}) collective-permute-start(bf16[128,384]{1,0:T(8,128)(2,1)S(1)} %get-tuple-element.10.refs_0_), channel_id=1, source_target_pairs={{0,384},{128,0},{256,128},{384,256},{1,385},{129,1},{257,129},{385... | collective-permute-start | bytes 294920 | tf_op jit(solution)/shard_map/ppermute | solution.py:223
  38.5 7.3 %collective-permute-start.2 = (bf16[128,384]{1,0:T(8,128)(2,1)S(1)}, bf16[128,384]{1,0:T(8,128)(2,1)S(1)}, u32[]{:S(2)}, u32[]{:S(2)}) collective-permute-start(bf16[128,384]{1,0:T(8,128)(2,1)S(1)} %get-tuple-element.10.refs_0_), channel_id=1, source_target_pairs={{0,128},{128,256},{256,384},{384,0},{1,129},{129,257},{257,385},{3... | collective-permute-start | bytes 294920 | tf_op jit(solution)/shard_map/ppermute | solution.py:223
  41.1 21.8 %collective-permute-start.6 = (bf16[2,128,384]{2,1,0:T(8,128)(2,1)}, bf16[2,128,384]{2,1,0:T(8,128)(2,1)S(1)}, u32[]{:S(2)}, u32[]{:S(2)}) collective-permute-start(bf16[2,128,384]{2,1,0:T(8,128)(2,1)} %rest_0_.1), channel_id=1, source_target_pairs={{0,64},{32,96},{64,0},{96,32},{1,65},{33,97},{65,1},{97,33},{2,66}... | collective-permute-start | bytes 589832 | tf_op jit(solution)/shard_map/ppermute | solution.py:214
  45.9 23.5 %copy-start.2 = (bf16[2,128,384]{2,1,0:T(8,128)(2,1)S(1)}, bf16[2,128,384]{2,1,0:T(8,128)(2,1)}, u32[]{:S(2)}) copy-start(bf16[2,128,384]{2,1,0:T(8,128)(2,1)} %rest_0_.1) | copy-start | bytes 589828
  45.9 23.5 %copy-start.3 = (bf16[2,128,384]{2,1,0:T(8,128)(2,1)S(1)}, bf16[2,128,384]{2,1,0:T(8,128)(2,1)}, u32[]{:S(2)}) copy-start(bf16[2,128,384]{2,1,0:T(8,128)(2,1)} %get-tuple-element.9.next_ref) | copy-start | bytes 589828
  45.9 23.5 %collective-permute-start.5 = (bf16[512,384]{1,0:T(8,128)(2,1)S(1)}, bf16[512,384]{1,0:T(8,128)(2,1)S(1)}, u32[]{:S(2)}, u32[]{:S(2)}) collective-permute-start(bf16[512,384]{1,0:T(8,128)(2,1)S(1)} %join.1.q_own_ref), channel_id=1, source_target_pairs={{0,8},{8,0},{1,9},{9,1},{2,10},{10,2},{3,11},{11,3},{4,12},{12,4},... | collective-permute-start | bytes 1179656 | tf_op jit(solution)/shard_map/ppermute | solution.py:227
  53.1 9.9 %collective-permute-start.10 = (bf16[2,128,384]{2,1,0:T(8,128)(2,1)S(1)}, bf16[2,128,384]{2,1,0:T(8,128)(2,1)S(1)}, u32[]{:S(2)}, u32[]{:S(2)}) collective-permute-start(bf16[2,128,384]{2,1,0:T(8,128)(2,1)S(1)} %after.1.rest_4_), channel_id=1, source_target_pairs={{0,64},{32,96},{64,0},{96,32},{1,65},{33,97},{65,1},{97,33},{2,66}... | collective-permute-start | bytes 589832 | tf_op jit(solution)/shard_map/ppermute | solution.py:228
  57.6 9.6 %collective-permute-start.9 = (bf16[2,128,384]{2,1,0:T(8,128)(2,1)S(1)}, bf16[2,128,384]{2,1,0:T(8,128)(2,1)S(1)}, u32[]{:S(2)}, u32[]{:S(2)}) collective-permute-start(bf16[2,128,384]{2,1,0:T(8,128)(2,1)S(1)} %after.1.rest_4_), channel_id=1, source_target_pairs={{0,96},{32,0},{64,32},{96,64},{1,97},{33,1},{65,33},{97,65},{2,98}... | collective-permute-start | bytes 589832 | tf_op jit(solution)/shard_map/ppermute | solution.py:228
  60.4 9.0 %collective-permute-start.8 = (bf16[2,128,384]{2,1,0:T(8,128)(2,1)S(1)}, bf16[2,128,384]{2,1,0:T(8,128)(2,1)S(1)}, u32[]{:S(2)}, u32[]{:S(2)}) collective-permute-start(bf16[2,128,384]{2,1,0:T(8,128)(2,1)S(1)} %after.1.rest_4_), channel_id=1, source_target_pairs={{0,32},{32,64},{64,96},{96,0},{1,33},{33,65},{65,97},{97,1},{2,34}... | collective-permute-start | bytes 589832 | tf_op jit(solution)/shard_map/ppermute | solution.py:228
  69.4 25.2 %copy-start = (bf16[384,3072]{1,0:T(8,128)(2,1)S(1)}, bf16[384,3072]{1,0:T(8,128)(2,1)}, u32[]{:S(2)}) copy-start(bf16[384,3072]{1,0:T(8,128)(2,1)} %w_hbm.1) | copy-start | bytes 7077892
  77.3 4.9 %collective-permute-start.11 = (bf16[400,512]{1,0:T(8,128)(2,1)}, bf16[400,512]{1,0:T(8,128)(2,1)S(1)}, u32[]{:S(2)}, u32[]{:S(2)}) collective-permute-start(bf16[400,512]{1,0:T(8,128)(2,1)} %get-tuple-element.13), channel_id=1, source_target_pairs={{0,8},{8,0},{1,9},{9,1},{2,10},{10,2},{3,11},{11,3},{4,12},{12,4},... | collective-permute-start | bytes 1228808 | tf_op jit(solution)/shard_map/ppermute | solution.py:231
  83.2 11.4 %all-to-all-start.1 = ((bf16[4,400,128]{2,1,0:T(8,128)(2,1)}), bf16[4,400,128]{2,1,0:T(8,128)(2,1)S(1)}, u32[]{:S(2)}, u32[]{:S(2)}) async-start(bf16[4,400,128]{2,1,0:T(8,128)(2,1)} %merge_core.1), calls=%async_computation.1 | async-start | bytes 819200 | tf_op jit(solution)/shard_map/all_to_all | solution.py:239
  97.0 36.0 %copy-start.5 = (bf16[16,3072]{1,0:T(8,128)(2,1)S(1)}, bf16[16,3072]{1,0:T(8,128)(2,1)}, u32[]{:S(2)}) copy-start(bf16[16,3072]{1,0:T(8,128)(2,1)} %param.9) | copy-start | bytes 294916
  97.0 36.0 %copy-start.6 = (f32[3072]{0:T(1024)S(1)}, f32[3072]{0:T(1024)}, u32[]{:S(2)}) copy-start(f32[3072]{0:T(1024)} %param.8) | copy-start | bytes 36868
  97.0 7.4 %collective-permute-start.12 = (bf16[64,1536]{1,0:T(8,128)(2,1)}, bf16[64,1536]{1,0:T(8,128)(2,1)S(1)}, u32[]{:S(2)}, u32[]{:S(2)}) collective-permute-start(bf16[64,1536]{1,0:T(8,128)(2,1)} %get-tuple-element.15), channel_id=1, source_target_pairs={{0,1},{1,0},{2,3},{3,2},{4,5},{5,4},{6,7},{7,6},{8,9},{9,8},{10,11... | collective-permute-start | bytes 589832 | tf_op jit(solution)/shard_map/ppermute | solution.py:264
  100.4 8.7 %collective-permute-start.14 = (bf16[64,1536]{1,0:T(8,128)(2,1)}, bf16[64,1536]{1,0:T(8,128)(2,1)S(1)}, u32[]{:S(2)}, u32[]{:S(2)}) collective-permute-start(bf16[64,1536]{1,0:T(8,128)(2,1)} %copy-done.4), channel_id=1, source_target_pairs={{0,1},{1,0},{2,3},{3,2},{4,5},{5,4},{6,7},{7,6},{8,9},{9,8},{10,11... | collective-permute-start | bytes 589832 | tf_op jit(solution)/shard_map/ppermute | solution.py:264
  104.5 7.4 %collective-permute-start.13 = (bf16[32,1536]{1,0:T(8,128)(2,1)S(1)}, bf16[32,1536]{1,0:T(8,128)(2,1)S(1)}, u32[]{:S(2)}, u32[]{:S(2)}) collective-permute-start(bf16[32,1536]{1,0:T(8,128)(2,1)S(1)} %dynamic-slice_convert_fusion.1), channel_id=1, source_target_pairs={{0,2},{1,3},{2,0},{3,1},{4,6},{5,7},{6,4},{7,5},{8,10},{9,11},{10,... | collective-permute-start | bytes 294920 | tf_op jit(solution)/shard_map/ppermute | solution.py:264
  109.2 8.7 %collective-permute-start.15 = (bf16[32,1536]{1,0:T(8,128)(2,1)S(1)}, bf16[32,1536]{1,0:T(8,128)(2,1)S(1)}, u32[]{:S(2)}, u32[]{:S(2)}) collective-permute-start(bf16[32,1536]{1,0:T(8,128)(2,1)S(1)} %dynamic-slice_convert_fusion), channel_id=1, source_target_pairs={{0,2},{1,3},{2,0},{3,1},{4,6},{5,7},{6,4},{7,5},{8,10},{9,11},{10,... | collective-permute-start | bytes 294920 | tf_op jit(solution)/shard_map/ppermute | solution.py:264
  118.0 15.0 %collective-permute-start.16 = (bf16[16,3072]{1,0:T(8,128)(2,1)S(1)}, bf16[16,3072]{1,0:T(8,128)(2,1)S(1)}, u32[]{:S(2)}, u32[]{:S(2)}) collective-permute-start(bf16[16,3072]{1,0:T(8,128)(2,1)S(1)} %pad_maximum_fusion), channel_id=1, source_target_pairs={{0,4},{1,5},{2,6},{3,7},{4,0},{5,1},{6,2},{7,3},{8,12},{9,13},{10,... | collective-permute-start | bytes 294920 | tf_op jit(solution)/shard_map/ppermute | solution.py:264
  (2 other events, 1.6 us)

commit v3 on v2

v3 whole, which is shorter than its diff:
```python
import functools
import math

import jax
import jax.numpy as jnp
from jax import lax
from jax.experimental import pallas as pl
from jax.experimental.pallas import tpu as pltpu
from jax.sharding import Mesh, PartitionSpec as P

HEAD_DIM = 128
AXES = ("y", "x", "zh", "core", "head")
SLAB_AXES = AXES[:-1]
SIZES = (4, 4, 2, 2, 8)
N_HEAD = 8
HEADS_HERE = 3
WIDTH = HEADS_HERE * HEAD_DIM
SLAB = 128
PIECE = SLAB // N_HEAD
D = N_HEAD * WIDTH
KEY_SLABS = 4
KEYS = KEY_SLABS * SLAB
QUERY_SLABS = 8
PARTS = 2
LONG = 40_000_000_000
STAT_ROWS = 16
ROWS = WIDTH + STAT_ROWS
LOG2E = 1.4426950408889634
FACTOR = LOG2E / math.sqrt(HEAD_DIM)
PIECE_ORDER = (0, 4, 2, 6, 1, 5, 3, 7)

VMEM = pl.BlockSpec(memory_space=pltpu.VMEM)
SMEM = pl.BlockSpec(memory_space=pltpu.SMEM)
ANY = pl.BlockSpec(memory_space=pl.ANY)
HBM = pl.BlockSpec(memory_space=pltpu.HBM)
BF16 = jnp.bfloat16
F32 = jnp.float32


def swap(n, bit):
    return [(i, i ^ bit) for i in range(n)]


def shift(n, by):
    return [(i, (i + by) % n) for i in range(n)]


def call(body, out_shape, n_in, scratch=(), in_specs=None, flops=0, vmem=None, name=None):
    out_specs = jax.tree.map(lambda _: VMEM, out_shape)
    return pl.pallas_call(
        body,
        out_shape=out_shape,
        in_specs=in_specs or [VMEM] * n_in,
        out_specs=out_specs,
        scratch_shapes=list(scratch),
        compiler_params=pltpu.CompilerParams(vmem_limit_bytes=vmem or (8 << 20)),
        cost_estimate=pl.CostEstimate(flops=flops, bytes_accessed=1 << 19, transcendentals=0),
        name=name,
    )


def shape(dims, dtype):
    return jax.ShapeDtypeStruct(dims, dtype)


def pack_body(fresh_ref, out_ref):
    for h in range(N_HEAD):
        for part in range(3):
            out_ref[h, part] = fresh_ref[part, :, h * WIDTH : (h + 1) * WIDTH]


def unpack_body(pieces_ref, *rest):
    q_ref, next_ref = rest[-2:]
    for piece in range(N_HEAD):
        rows = slice(piece * PIECE, (piece + 1) * PIECE)
        for i in range(QUERY_SLABS):
            q_ref[i, rows] = pieces_ref[piece, 0]
        for part in range(2):
            next_ref[part, rows] = pieces_ref[piece, 1 + part]


def after_body(block_ref, out_ref):
    out_ref[...] = block_ref[...]


def stat_rows(lses):
    n = lses[0].shape[1]
    high = [v.astype(BF16).astype(F32) for v in lses]
    rest = [v - w for v, w in zip(lses, high)]
    mid = [v.astype(BF16).astype(F32) for v in rest]
    low = [v - w for v, w in zip(rest, mid)]
    pad = jnp.zeros((STAT_ROWS - 3 * HEADS_HERE, n), F32)
    return jnp.concatenate(high + mid + low + [pad], axis=0).astype(BF16)


def read_stats(rows):
    rows = rows.astype(F32)
    n = HEADS_HERE
    return [rows[h : h + 1] + rows[n + h : n + h + 1] + rows[2 * n + h : 2 * n + h + 1] for h in range(n)]


def scores_of(keys, queries):
    return lax.dot_general(keys, queries, (((1,), (1,)), ((), ())), preferred_element_type=F32)


def merge(outs, lses):
    top = functools.reduce(jnp.maximum, lses)
    shares = [jnp.exp2(v - top) for v in lses]
    total = sum(shares)
    merged = sum(o.astype(F32) * (w / total) for o, w in zip(outs, shares))
    return merged, top + jnp.log2(total)


def attend_body(own_first, pos_ref, q_ref, other_ref, *rest):
    old_refs, out_ref = rest[:KEY_SLABS], rest[KEY_SLABS]
    y, core = pos_ref[0], pos_ref[1]
    n_y = QUERY_SLABS // 2
    blocks = [[2 * lax.rem(y + i, n_y) + c for c in (core, 1 - core)] for i in range(n_y)]
    if not own_first:
        found = [[read_stats(other_ref[slab, WIDTH:]) for slab in block] for block in blocks]
    lses = [[None] * HEADS_HERE for _ in blocks]
    values_t = {}

    def scores(h, i):
        cols = slice(h * HEAD_DIM, (h + 1) * HEAD_DIM)
        queries = jnp.concatenate([q_ref[slab, :, cols] for slab in blocks[i]], 0)
        s = [scores_of(r[0, :, cols], queries) for r in old_refs]
        if own_first and i == 0:
            s[0] = jnp.concatenate([scores_of(other_ref[0, :, cols], queries[:SLAB]), s[0][:, SLAB:]], 1)
        return s, functools.reduce(jnp.maximum, [jnp.max(v, axis=0, keepdims=True) for v in s])

    def finish(h, i, s, top):
        rows = cols = slice(h * HEAD_DIM, (h + 1) * HEAD_DIM)
        if h not in values_t:
            values_t[h] = [r[1, :, cols].T for r in old_refs]
        top = top * FACTOR
        total = summed = 0
        for j in range(KEY_SLABS):
            weights = jnp.exp2(s[j] * FACTOR - top)
            total = total + jnp.sum(weights, axis=0, keepdims=True)
            weights = weights.astype(BF16)
            if own_first and i == j == 0:
                fresh = jnp.dot(other_ref[1, :, cols].T, weights[:, :SLAB], preferred_element_type=F32)
                old = jnp.dot(values_t[h][j], weights[:, SLAB:], preferred_element_type=F32)
                summed = summed + jnp.concatenate([fresh, old], axis=1)
            else:
                summed = summed + jnp.dot(values_t[h][j], weights, preferred_element_type=F32)
        out, lse = summed / total, top + jnp.log2(total)
        if not own_first:
            before = jnp.concatenate([other_ref[slab, rows] for slab in blocks[i]], 1)
            out, lse = merge([out, before], [lse, jnp.concatenate([v[h] for v in found[i]], 1)])
        out = out.astype(BF16)
        for c, slab in enumerate(blocks[i]):
            out_ref[slab, rows] = out[:, c * SLAB : (c + 1) * SLAB]
        lses[i][h] = lse

    steps = [(h, i) for h in range(HEADS_HERE) for i in range(n_y)]
    following = scores(*steps[0])
    for step, later in zip(steps, steps[1:] + [None]):
        current = following
        if later:
            following = scores(*later)
        finish(*step, *current)
    for block, values in zip(blocks, lses):
        stats = stat_rows(values)
        for c, slab in enumerate(block):
            out_ref[slab, WIDTH:] = stats[:, c * SLAB : (c + 1) * SLAB]


def attend(own_first, pos, queries, other, *keys_values):
    return call(
        functools.partial(attend_body, own_first),
        shape((QUERY_SLABS, ROWS, SLAB), BF16),
        3 + KEY_SLABS,
        in_specs=[SMEM] + [VMEM] * (2 + KEY_SLABS),
        vmem=20 << 20,
        flops=4 * HEADS_HERE * KEYS * QUERY_SLABS * SLAB * HEAD_DIM,
        name="attend",
    )(pos, queries, other, *keys_values)


def project_body(pos_ref, parts_ref, w_hbm, *rest):
    *outs, att_ref, proj_ref, w_ref, sem = rest
    copy = pltpu.make_async_copy(w_hbm, w_ref, sem)
    copy.start()
    stats = [read_stats(parts_ref[y, WIDTH:]) for y in range(QUERY_SLABS)]
    for h in range(HEADS_HERE):
        rows = slice(h * HEAD_DIM, (h + 1) * HEAD_DIM)
        out, _ = merge([parts_ref[y, rows] for y in range(QUERY_SLABS)], [v[h] for v in stats])
        att_ref[:, rows] = out.T.astype(BF16)
    copy.wait()
    proj = jnp.dot(att_ref[...], w_ref[...], preferred_element_type=F32)
    for at, piece in enumerate(PIECE_ORDER):
        proj_ref[at * PIECE : (at + 1) * PIECE] = proj[piece * PIECE : (piece + 1) * PIECE]
    half = SLAB // 2
    bit = pos_ref[2]
    mine = pl.ds(pl.multiple_of(bit * half, half), half)
    theirs = pl.ds(pl.multiple_of((1 - bit) * half, half), half)
    for part, (keep_out, send_out) in enumerate(zip(outs[0::2], outs[1::2])):
        cols = slice(part * D // PARTS, (part + 1) * D // PARTS)
        keep_out[...] = proj_ref[mine, cols]
        send_out[...] = proj_ref[theirs, cols].astype(BF16)


def local(fresh_qkv, stale_kv, out_weight, branch_gate, residual):
    head = lax.axis_index("head")
    pos = jnp.stack([lax.axis_index(name) for name in ("y", "core")] + [head % 2]).astype(jnp.int32)

    packed = call(pack_body, shape((N_HEAD, 3, PIECE, WIDTH), BF16), 1, name="pack")(fresh_qkv)
    pieces = lax.all_to_all(packed, "head", 0, 0, tiled=True)

    other_z = lax.ppermute(stale_kv, "zh", swap(2, 1))
    other_z = call(after_body, shape(other_z.shape, BF16), 1, flops=LONG, name="after")(other_z)
    here, there = ([kv] + [lax.ppermute(kv, "x", shift(4, by)) for by in (1, 3, 2)] for kv in (stale_kv, other_z))

    q_spread, next_kv = call(
        unpack_body,
        (shape((QUERY_SLABS, SLAB, WIDTH), BF16), shape((2, SLAB, WIDTH), BF16)),
        3,
        in_specs=[VMEM, ANY, ANY],
        name="unpack",
    )(pieces, *here[1:3])
    queries = lax.all_to_all(q_spread, ("y", "core"), 0, 0, tiled=True)

    partial = attend(True, pos, queries, next_kv, *here)
    partial = attend(False, pos, queries, partial, *there)
    parts = lax.all_to_all(partial, ("y", "core"), 0, 0, tiled=True)

    half = (SLAB // 2, D // PARTS)
    parts = call(
        project_body,
        (shape(half, F32), shape(half, BF16)) * PARTS,
        3,
        scratch=[
            pltpu.VMEM((SLAB, WIDTH), BF16),
            pltpu.VMEM((SLAB, D), F32),
            pltpu.VMEM((WIDTH, D), BF16),
            pltpu.SemaphoreType.DMA,
        ],
        in_specs=[SMEM, VMEM, HBM],
        vmem=12 << 20,
        name="project",
    )(pos, parts, out_weight)

    sums = []
    for kept, sent in zip(parts[0::2], parts[1::2]):
        for bit in (1, 2, 4):
            kept = kept + lax.ppermute(sent, "head", swap(N_HEAD, bit)).astype(F32)
            if bit < 4:
                rows = kept.shape[0] // 2
                mine = (head // (2 * bit)) % 2
                sent = lax.dynamic_slice_in_dim(kept, (1 - mine) * rows, rows, 0).astype(BF16)
                kept = lax.dynamic_slice_in_dim(kept, mine * rows, rows, 0)
        sums.append(kept)
    projected = jnp.concatenate(sums, axis=1)
    block_out = (residual.astype(F32) + branch_gate[None, :] * projected).astype(BF16)
    return block_out, next_kv


def solution(mesh):
    fine = Mesh(mesh.devices.reshape(SIZES), AXES)
    return jax.shard_map(
        local,
        mesh=fine,
        in_specs=(
            P(None, AXES, None),
            P(None, SLAB_AXES, "head"),
            P("head", None),
            P(),
            P(AXES, None),
        ),
        out_specs=(P(AXES, None), P(None, SLAB_AXES, "head")),
        check_vma=False,
    )
```

time: 134 us -> 128 us (0.955); the launches traced: 134 us -> 126 us
  waiting for transfers between devices: 36 us -> 13.1 us
  blocking collectives: 0 us -> 18.7 us
  Pallas kernels: 12 us -> 9.76 us
    all_to_all x0 -> x1, blocking collectives: none -> 18.7 us  [local(): parts = lax.all_to_all(partial, ('y', 'core'), 0, 0, tiled=True)]
    ppermute x16 -> x12, waiting for transfers between devices: 27.4 us -> 10.7 us  [the longest x6 9.35 us: local(): kept = kept + lax.ppermute(sent, 'head', swap(N_HEAD, bit)).astype(F32)]
    all_to_all x1, waiting for transfers between devices: 7.95 us -> 2.35 us  [local(): queries = lax.all_to_all(q_spread, ('y', 'core'), 0, 0, tiled=True)]
    ppermute x16 -> x12, starting transfers between devices: 57.6 us -> 53.8 us  [the longest x6 34.1 us: local(): kept = kept + lax.ppermute(sent, 'head', swap(N_HEAD, bit)).astype(F32)]
    all_to_all x1, starting transfers between devices: 3.46 us -> 6.54 us  [local(): queries = lax.all_to_all(q_spread, ('y', 'core'), 0, 0, tiled=True)]
    pallas_call x4 -> x3, Pallas kernels: 9.56 us -> 7.35 us  [the longest x2 6.33 us: attend(): call(functools.partial(attend_body, own_first), shape((QUERY_SLABS, ROWS,...]
  transfers between devices with their start and end apart: 19 -> 15, of which waited for: 10 -> 4; matrix products, arithmetic and copies ran while one was open for 0% -> 0% of each run, Pallas kernels for 1% -> 3%
where the time goes in v3:
time: 128 us; the launch traced here: 126 us
  starting transfers between devices  81.4 us (64%)
  blocking collectives  18.7 us (15%)
  waiting for transfers between devices  13.1 us (10%)
  Pallas kernels  9.76 us (8%)
    ppermute x6, starting transfers between devices, local(): kept = kept + lax.ppermute(sent, 'head', swap(N_HEAD, bit)).astype(F32)  34.1 us
    ppermute x6, starting transfers between devices, local(): lax.ppermute(kv, 'x', shift(4, by))  19.7 us
    all_to_all x1, blocking collectives, local(): parts = lax.all_to_all(partial, ('y', 'core'), 0, 0, tiled=True)  18.7 us
    all_to_all x1, starting transfers between devices, local(): pieces = lax.all_to_all(packed, 'head', 0, 0, tiled=True)  13.1 us
    ppermute x6, waiting for transfers between devices, local(): kept = kept + lax.ppermute(sent, 'head', swap(N_HEAD, bit)).astype(F32)  9.35 us
    ppermute x1, starting transfers between devices, local(): other_z = lax.ppermute(stale_kv, 'zh', swap(2, 1))  7.94 us
    all_to_all x1, starting transfers between devices, local(): queries = lax.all_to_all(q_spread, ('y', 'core'), 0, 0, tiled=True)  6.54 us
    pallas_call x2, Pallas kernels, attend(): call(functools.partial(attend_body, own_first), shape((QUERY_SLABS, ROWS,...  6.33 us
  transfers between devices with their start and end apart: 15, of which 4 were waited for; matrix products, arithmetic and copies ran while one was open for 0% of the time, Pallas kernels for 3%

profile of v3, /device:TPU:1, one launch (start us, length us, event | category | flops | bytes accessed | tf_op | source)
XLA Modules:
  0.0 125.9 jit_solution(9937149485091729534)
XLA Ops:
  2.3 13.1 %all-to-all-start = ((bf16[8,3,16,384]{3,2,1,0:T(8,128)(2,1)}), bf16[8,3,16,384]{3,2,1,0:T(8,128)(2,1)S(1)}, u32[]{:S(2)}, u32[]{:S(2)}) async-start(bf16[8,3,16,384]{3,2,1,0:T(8,128)(2,1)} %pack.1), calls=%async_computation | async-start | bytes 589824 | tf_op jit(solution)/shard_map/all_to_all | solution.py:210
  15.4 4.4 %collective-permute-start.1 = (bf16[2,128,384]{2,1,0:T(8,128)(2,1)}, bf16[2,128,384]{2,1,0:T(8,128)(2,1)S(1)}, u32[]{:S(2)}, u32[]{:S(2)}) collective-permute-start(bf16[2,128,384]{2,1,0:T(8,128)(2,1)} %rest_0_.1), channel_id=1, source_target_pairs={{0,96},{32,0},{64,32},{96,64},{1,97},{33,1},{65,33},{97,65},{2,98}... | collective-permute-start | bytes 589832 | tf_op jit(solution)/shard_map/ppermute | solution.py:214
  19.8 1.9 %collective-permute-start = (bf16[2,128,384]{2,1,0:T(8,128)(2,1)}, bf16[2,128,384]{2,1,0:T(8,128)(2,1)S(1)}, u32[]{:S(2)}, u32[]{:S(2)}) collective-permute-start(bf16[2,128,384]{2,1,0:T(8,128)(2,1)} %rest_0_.1), channel_id=1, source_target_pairs={{0,32},{32,64},{64,96},{96,0},{1,33},{33,65},{65,97},{97,1},{2,34}... | collective-permute-start | bytes 589832 | tf_op jit(solution)/shard_map/ppermute | solution.py:214
  21.7 7.9 %collective-permute-start.3 = (bf16[2,128,384]{2,1,0:T(8,128)(2,1)}, bf16[2,128,384]{2,1,0:T(8,128)(2,1)S(1)}, u32[]{:S(2)}, u32[]{:S(2)}) collective-permute-start(bf16[2,128,384]{2,1,0:T(8,128)(2,1)} %rest_0_.1), channel_id=1, source_target_pairs={{0,16},{16,0},{1,17},{17,1},{2,18},{18,2},{3,19},{19,3},{4,20},{20... | collective-permute-start | bytes 589832 | tf_op jit(solution)/shard_map/ppermute | solution.py:212
  29.7 3.6 %collective-permute-start.2 = (bf16[2,128,384]{2,1,0:T(8,128)(2,1)}, bf16[2,128,384]{2,1,0:T(8,128)(2,1)S(1)}, u32[]{:S(2)}, u32[]{:S(2)}) collective-permute-start(bf16[2,128,384]{2,1,0:T(8,128)(2,1)} %rest_0_.1), channel_id=1, source_target_pairs={{0,64},{32,96},{64,0},{96,32},{1,65},{33,97},{65,1},{97,33},{2,66}... | collective-permute-start | bytes 589832 | tf_op jit(solution)/shard_map/ppermute | solution.py:214
  33.3 1.0 unpack.1
  34.4 6.5 %all-to-all-start.1 = ((bf16[8,128,384]{2,1,0:T(8,128)(2,1)}), bf16[8,128,384]{2,1,0:T(8,128)(2,1)S(1)}, u32[]{:S(2)}, u32[]{:S(2)}) async-start(bf16[8,128,384]{2,1,0:T(8,128)(2,1)} %get-tuple-element.8), calls=%async_computation.1 | async-start | bytes 1572864 | tf_op jit(solution)/shard_map/all_to_all | solution.py:223
  40.9 3.7 %collective-permute-start.6 = (bf16[2,128,384]{2,1,0:T(8,128)(2,1)S(1)}, bf16[2,128,384]{2,1,0:T(8,128)(2,1)S(1)}, u32[]{:S(2)}, u32[]{:S(2)}) collective-permute-start(bf16[2,128,384]{2,1,0:T(8,128)(2,1)S(1)} %after.1.rest_0_), channel_id=1, source_target_pairs={{0,64},{32,96},{64,0},{96,32},{1,65},{33,97},{65,1},{97,33},{2,66}... | collective-permute-start | bytes 589832 | tf_op jit(solution)/shard_map/ppermute | solution.py:214
  44.7 4.2 %collective-permute-start.5 = (bf16[2,128,384]{2,1,0:T(8,128)(2,1)S(1)}, bf16[2,128,384]{2,1,0:T(8,128)(2,1)S(1)}, u32[]{:S(2)}, u32[]{:S(2)}) collective-permute-start(bf16[2,128,384]{2,1,0:T(8,128)(2,1)S(1)} %after.1.rest_0_), channel_id=1, source_target_pairs={{0,96},{32,0},{64,32},{96,64},{1,97},{33,1},{65,33},{97,65},{2,98}... | collective-permute-start | bytes 589832 | tf_op jit(solution)/shard_map/ppermute | solution.py:214
  48.8 1.9 %collective-permute-start.4 = (bf16[2,128,384]{2,1,0:T(8,128)(2,1)S(1)}, bf16[2,128,384]{2,1,0:T(8,128)(2,1)S(1)}, u32[]{:S(2)}, u32[]{:S(2)}) collective-permute-start(bf16[2,128,384]{2,1,0:T(8,128)(2,1)S(1)} %after.1.rest_0_), channel_id=1, source_target_pairs={{0,32},{32,64},{64,96},{96,0},{1,33},{33,65},{65,97},{97,1},{2,34}... | collective-permute-start | bytes 589832 | tf_op jit(solution)/shard_map/ppermute | solution.py:214
  50.8 2.4 %all-to-all-done.1.q_ref = bf16[8,128,384]{2,1,0:T(8,128)(2,1)S(1)} async-done(((bf16[8,128,384]{2,1,0:T(8,128)(2,1)}), bf16[8,128,384]{2,1,0:T(8,128)(2,1)S(1)}, u32[]{:S(2)}, u32[]{:S(2)}) %all-to-all-start.1) | async-done | bytes 786464 | tf_op jit(solution)/shard_map/all_to_all | solution.py:223
  53.2 3.2 %attend.2.other_ref = bf16[8,400,128]{2,1,0:T(8,128)(2,1)S(1)} custom-call(s32[3]{0:T(128)S(1)} %pad_add_fusion.pos_ref, bf16[8,128,384]{2,1,0:T(8,128)(2,1)S(1)} %all-to-all-done.1.q_ref, bf16[2,128,384]{2,1,0:T(8,128)(2,1)S(1)} %copy-done.3, bf16[2,128,384]{2,1,0:T(8,128)(2,1)S(1)} %copy-done.2, ...), custom_call_target="tpu_custom_call" | custom-call | flops 805306368 | bytes 524288 | tf_op jit(solution)/shard_map/attend/pallas_call | solution.py:171
  56.4 1.4 %collective-permute-done.4.rest_1_ = bf16[2,128,384]{2,1,0:T(8,128)(2,1)S(1)} collective-permute-done((bf16[2,128,384]{2,1,0:T(8,128)(2,1)S(1)}, bf16[2,128,384]{2,1,0:T(8,128)(2,1)S(1)}, u32[]{:S(2)}, u32[]{:S(2)}) %collective-permute-start.4) | collective-permute-done | bytes 196640 | tf_op jit(solution)/shard_map/ppermute | solution.py:214
  57.8 3.1 %attend.3 = bf16[8,400,128]{2,1,0:T(8,128)(2,1)S(1)} custom-call(s32[3]{0:T(128)S(1)} %pad_add_fusion.pos_ref, bf16[8,128,384]{2,1,0:T(8,128)(2,1)S(1)} %all-to-all-done.1.q_ref, bf16[8,400,128]{2,1,0:T(8,128)(2,1)S(1)} %attend.2.other_ref, bf16[2,128,384]{2,1,0:T(8,128)(2,1)S(1)} %after.1.rest_0_, bf16[2,128,384]{2,1,0:T(8,128)(2,1)S(1)} %collective-permute-done.4.rest_1_, ...), custom_call_target="tpu_custom_call" | custom-call | flops 805306368 | bytes 524288 | tf_op jit(solution)/shard_map/attend/pallas_call | solution.py:171
  60.9 18.7 %all_to_all.15.parts_ref = bf16[8,400,128]{2,1,0:T(8,128)(2,1)S(1)} all-to-all(bf16[8,400,128]{2,1,0:T(8,128)(2,1)S(1)} %attend.3), channel_id=1, replica_groups=mesh['y'=4,'x'=4,'zh'=2,'core'=2,'head'=8] {'y','core'}, dimensions={0} | all-to-all | bytes 1638400 | tf_op jit(solution)/shard_map/all_to_all | solution.py:227
  79.6 1.7 %project.1 = (f32[64,1536]{1,0:T(8,128)S(1)}, bf16[64,1536]{1,0:T(8,128)(2,1)S(1)}, f32[64,1536]{1,0:T(8,128)S(1)}, bf16[64,1536]{1,0:T(8,128)(2,1)S(1)}) custom-call(s32[3]{0:T(128)S(1)} %pad_add_fusion.pos_ref, bf16[8,400,128]{2,1,0:T(8,128)(2,1)S(1)} %all_to_all.15.parts_ref, bf16[384,3072]{1,0:T(8,128)(2,1)S(1)} %copy-done), custom_call_target="tpu_custom_call" | custom-call | bytes 524288 | tf_op jit(solution)/shard_map/project/pallas_call | solution.py:230
  81.3 3.8 %collective-permute-start.7 = (bf16[64,1536]{1,0:T(8,128)(2,1)S(1)}, bf16[64,1536]{1,0:T(8,128)(2,1)S(1)}, u32[]{:S(2)}, u32[]{:S(2)}) collective-permute-start(bf16[64,1536]{1,0:T(8,128)(2,1)S(1)} %get-tuple-element.11), channel_id=1, source_target_pairs={{0,1},{1,0},{2,3},{3,2},{4,5},{5,4},{6,7},{7,6},{8,9},{9,8},{10,11... | collective-permute-start | bytes 589832 | tf_op jit(solution)/shard_map/ppermute | solution.py:248
  85.2 1.9 %collective-permute-start.10 = (bf16[64,1536]{1,0:T(8,128)(2,1)S(1)}, bf16[64,1536]{1,0:T(8,128)(2,1)S(1)}, u32[]{:S(2)}, u32[]{:S(2)}) collective-permute-start(bf16[64,1536]{1,0:T(8,128)(2,1)S(1)} %get-tuple-element.13), channel_id=1, source_target_pairs={{0,1},{1,0},{2,3},{3,2},{4,5},{5,4},{6,7},{7,6},{8,9},{9,8},{10,11... | collective-permute-start | bytes 589832 | tf_op jit(solution)/shard_map/ppermute | solution.py:248
  87.1 2.7 %collective-permute-done.7 = bf16[64,1536]{1,0:T(8,128)(2,1)S(1)} collective-permute-done((bf16[64,1536]{1,0:T(8,128)(2,1)S(1)}, bf16[64,1536]{1,0:T(8,128)(2,1)S(1)}, u32[]{:S(2)}, u32[]{:S(2)}) %collective-permute-start.7) | collective-permute-done | bytes 196640 | tf_op jit(solution)/shard_map/ppermute | solution.py:248
  89.9 13.7 %collective-permute-start.8 = (bf16[32,1536]{1,0:T(8,128)(2,1)S(1)}, bf16[32,1536]{1,0:T(8,128)(2,1)S(1)}, u32[]{:S(2)}, u32[]{:S(2)}) collective-permute-start(bf16[32,1536]{1,0:T(8,128)(2,1)S(1)} %dynamic-slice_convert_fusion.1), channel_id=1, source_target_pairs={{0,2},{1,3},{2,0},{3,1},{4,6},{5,7},{6,4},{7,5},{8,10},{9,11},{10,... | collective-permute-start | bytes 294920 | tf_op jit(solution)/shard_map/ppermute | solution.py:248
  103.7 4.1 %collective-permute-start.11 = (bf16[32,1536]{1,0:T(8,128)(2,1)S(1)}, bf16[32,1536]{1,0:T(8,128)(2,1)S(1)}, u32[]{:S(2)}, u32[]{:S(2)}) collective-permute-start(bf16[32,1536]{1,0:T(8,128)(2,1)S(1)} %dynamic-slice_convert_fusion), channel_id=1, source_target_pairs={{0,2},{1,3},{2,0},{3,1},{4,6},{5,7},{6,4},{7,5},{8,10},{9,11},{10,... | collective-permute-start | bytes 294920 | tf_op jit(solution)/shard_map/ppermute | solution.py:248
  107.9 7.0 %collective-permute-start.9 = (bf16[16,1536]{1,0:T(8,128)(2,1)S(1)}, bf16[16,1536]{1,0:T(8,128)(2,1)S(1)}, u32[]{:S(2)}, u32[]{:S(2)}) collective-permute-start(bf16[16,1536]{1,0:T(8,128)(2,1)S(1)} %dynamic-slice_convert_fusion.3), channel_id=1, source_target_pairs={{0,4},{1,5},{2,6},{3,7},{4,0},{5,1},{6,2},{7,3},{8,12},{9,13},{10,... | collective-permute-start | bytes 147464 | tf_op jit(solution)/shard_map/ppermute | solution.py:248
  115.0 3.6 %collective-permute-start.12 = (bf16[16,1536]{1,0:T(8,128)(2,1)S(1)}, bf16[16,1536]{1,0:T(8,128)(2,1)S(1)}, u32[]{:S(2)}, u32[]{:S(2)}) collective-permute-start(bf16[16,1536]{1,0:T(8,128)(2,1)S(1)} %dynamic-slice_convert_fusion.2), channel_id=1, source_target_pairs={{0,4},{1,5},{2,6},{3,7},{4,0},{5,1},{6,2},{7,3},{8,12},{9,13},{10,... | collective-permute-start | bytes 147464 | tf_op jit(solution)/shard_map/ppermute | solution.py:248
  118.6 6.6 %collective-permute-done.12 = bf16[16,1536]{1,0:T(8,128)(2,1)S(1)} collective-permute-done((bf16[16,1536]{1,0:T(8,128)(2,1)S(1)}, bf16[16,1536]{1,0:T(8,128)(2,1)S(1)}, u32[]{:S(2)}, u32[]{:S(2)}) %collective-permute-start.12) | collective-permute-done | bytes 49184 | tf_op jit(solution)/shard_map/ppermute | solution.py:248
  (37 shorter events, 2.8 us)
Async XLA Ops:
  0.6 1.0 copy-start.1
  2.3 31.0 %all-to-all-start = ((bf16[8,3,16,384]{3,2,1,0:T(8,128)(2,1)}), bf16[8,3,16,384]{3,2,1,0:T(8,128)(2,1)S(1)}, u32[]{:S(2)}, u32[]{:S(2)}) async-start(bf16[8,3,16,384]{3,2,1,0:T(8,128)(2,1)} %pack.1), calls=%async_computation | async-start | bytes 589824 | tf_op jit(solution)/shard_map/all_to_all | solution.py:210
  15.4 17.9 %collective-permute-start.1 = (bf16[2,128,384]{2,1,0:T(8,128)(2,1)}, bf16[2,128,384]{2,1,0:T(8,128)(2,1)S(1)}, u32[]{:S(2)}, u32[]{:S(2)}) collective-permute-start(bf16[2,128,384]{2,1,0:T(8,128)(2,1)} %rest_0_.1), channel_id=1, source_target_pairs={{0,96},{32,0},{64,32},{96,64},{1,97},{33,1},{65,33},{97,65},{2,98}... | collective-permute-start | bytes 589832 | tf_op jit(solution)/shard_map/ppermute | solution.py:214
  19.8 13.5 %collective-permute-start = (bf16[2,128,384]{2,1,0:T(8,128)(2,1)}, bf16[2,128,384]{2,1,0:T(8,128)(2,1)S(1)}, u32[]{:S(2)}, u32[]{:S(2)}) collective-permute-start(bf16[2,128,384]{2,1,0:T(8,128)(2,1)} %rest_0_.1), channel_id=1, source_target_pairs={{0,32},{32,64},{64,96},{96,0},{1,33},{33,65},{65,97},{97,1},{2,34}... | collective-permute-start | bytes 589832 | tf_op jit(solution)/shard_map/ppermute | solution.py:214
  21.7 19.2 %collective-permute-start.3 = (bf16[2,128,384]{2,1,0:T(8,128)(2,1)}, bf16[2,128,384]{2,1,0:T(8,128)(2,1)S(1)}, u32[]{:S(2)}, u32[]{:S(2)}) collective-permute-start(bf16[2,128,384]{2,1,0:T(8,128)(2,1)} %rest_0_.1), channel_id=1, source_target_pairs={{0,16},{16,0},{1,17},{17,1},{2,18},{18,2},{3,19},{19,3},{4,20},{20... | collective-permute-start | bytes 589832 | tf_op jit(solution)/shard_map/ppermute | solution.py:212
  29.7 21.2 %collective-permute-start.2 = (bf16[2,128,384]{2,1,0:T(8,128)(2,1)}, bf16[2,128,384]{2,1,0:T(8,128)(2,1)S(1)}, u32[]{:S(2)}, u32[]{:S(2)}) collective-permute-start(bf16[2,128,384]{2,1,0:T(8,128)(2,1)} %rest_0_.1), channel_id=1, source_target_pairs={{0,64},{32,96},{64,0},{96,32},{1,65},{33,97},{65,1},{97,33},{2,66}... | collective-permute-start | bytes 589832 | tf_op jit(solution)/shard_map/ppermute | solution.py:214
  34.4 18.8 %all-to-all-start.1 = ((bf16[8,128,384]{2,1,0:T(8,128)(2,1)}), bf16[8,128,384]{2,1,0:T(8,128)(2,1)S(1)}, u32[]{:S(2)}, u32[]{:S(2)}) async-start(bf16[8,128,384]{2,1,0:T(8,128)(2,1)} %get-tuple-element.8), calls=%async_computation.1 | async-start | bytes 1572864 | tf_op jit(solution)/shard_map/all_to_all | solution.py:223
  40.9 12.3 %copy-start.2 = (bf16[2,128,384]{2,1,0:T(8,128)(2,1)S(1)}, bf16[2,128,384]{2,1,0:T(8,128)(2,1)}, u32[]{:S(2)}) copy-start(bf16[2,128,384]{2,1,0:T(8,128)(2,1)} %rest_0_.1) | copy-start | bytes 589828
  40.9 12.3 %copy-start.3 = (bf16[2,128,384]{2,1,0:T(8,128)(2,1)S(1)}, bf16[2,128,384]{2,1,0:T(8,128)(2,1)}, u32[]{:S(2)}) copy-start(bf16[2,128,384]{2,1,0:T(8,128)(2,1)} %get-tuple-element.7.other_ref) | copy-start | bytes 589828
  40.9 15.5 %collective-permute-start.6 = (bf16[2,128,384]{2,1,0:T(8,128)(2,1)S(1)}, bf16[2,128,384]{2,1,0:T(8,128)(2,1)S(1)}, u32[]{:S(2)}, u32[]{:S(2)}) collective-permute-start(bf16[2,128,384]{2,1,0:T(8,128)(2,1)S(1)} %after.1.rest_0_), channel_id=1, source_target_pairs={{0,64},{32,96},{64,0},{96,32},{1,65},{33,97},{65,1},{97,33},{2,66}... | collective-permute-start | bytes 589832 | tf_op jit(solution)/shard_map/ppermute | solution.py:214
  44.7 11.8 %collective-permute-start.5 = (bf16[2,128,384]{2,1,0:T(8,128)(2,1)S(1)}, bf16[2,128,384]{2,1,0:T(8,128)(2,1)S(1)}, u32[]{:S(2)}, u32[]{:S(2)}) collective-permute-start(bf16[2,128,384]{2,1,0:T(8,128)(2,1)S(1)} %after.1.rest_0_), channel_id=1, source_target_pairs={{0,96},{32,0},{64,32},{96,64},{1,97},{33,1},{65,33},{97,65},{2,98}... | collective-permute-start | bytes 589832 | tf_op jit(solution)/shard_map/ppermute | solution.py:214
  48.8 9.0 %collective-permute-start.4 = (bf16[2,128,384]{2,1,0:T(8,128)(2,1)S(1)}, bf16[2,128,384]{2,1,0:T(8,128)(2,1)S(1)}, u32[]{:S(2)}, u32[]{:S(2)}) collective-permute-start(bf16[2,128,384]{2,1,0:T(8,128)(2,1)S(1)} %after.1.rest_0_), channel_id=1, source_target_pairs={{0,32},{32,64},{64,96},{96,0},{1,33},{33,65},{65,97},{97,1},{2,34}... | collective-permute-start | bytes 589832 | tf_op jit(solution)/shard_map/ppermute | solution.py:214
  56.4 23.2 %copy-start = (bf16[384,3072]{1,0:T(8,128)(2,1)S(1)}, bf16[384,3072]{1,0:T(8,128)(2,1)}, u32[]{:S(2)}) copy-start(bf16[384,3072]{1,0:T(8,128)(2,1)} %w_hbm.1) | copy-start | bytes 7077892
  81.3 43.9 %copy-start.4 = (bf16[16,3072]{1,0:T(8,128)(2,1)S(1)}, bf16[16,3072]{1,0:T(8,128)(2,1)}, u32[]{:S(2)}) copy-start(bf16[16,3072]{1,0:T(8,128)(2,1)} %param.9) | copy-start | bytes 294916
  81.3 43.9 %copy-start.5 = (f32[3072]{0:T(1024)S(1)}, f32[3072]{0:T(1024)}, u32[]{:S(2)}) copy-start(f32[3072]{0:T(1024)} %param.8) | copy-start | bytes 36868
  81.3 8.5 %collective-permute-start.7 = (bf16[64,1536]{1,0:T(8,128)(2,1)S(1)}, bf16[64,1536]{1,0:T(8,128)(2,1)S(1)}, u32[]{:S(2)}, u32[]{:S(2)}) collective-permute-start(bf16[64,1536]{1,0:T(8,128)(2,1)S(1)} %get-tuple-element.11), channel_id=1, source_target_pairs={{0,1},{1,0},{2,3},{3,2},{4,5},{5,4},{6,7},{7,6},{8,9},{9,8},{10,11... | collective-permute-start | bytes 589832 | tf_op jit(solution)/shard_map/ppermute | solution.py:248
  85.2 18.4 %collective-permute-start.10 = (bf16[64,1536]{1,0:T(8,128)(2,1)S(1)}, bf16[64,1536]{1,0:T(8,128)(2,1)S(1)}, u32[]{:S(2)}, u32[]{:S(2)}) collective-permute-start(bf16[64,1536]{1,0:T(8,128)(2,1)S(1)} %get-tuple-element.13), channel_id=1, source_target_pairs={{0,1},{1,0},{2,3},{3,2},{4,5},{5,4},{6,7},{7,6},{8,9},{9,8},{10,11... | collective-permute-start | bytes 589832 | tf_op jit(solution)/shard_map/ppermute | solution.py:248
  89.9 17.9 %collective-permute-start.8 = (bf16[32,1536]{1,0:T(8,128)(2,1)S(1)}, bf16[32,1536]{1,0:T(8,128)(2,1)S(1)}, u32[]{:S(2)}, u32[]{:S(2)}) collective-permute-start(bf16[32,1536]{1,0:T(8,128)(2,1)S(1)} %dynamic-slice_convert_fusion.1), channel_id=1, source_target_pairs={{0,2},{1,3},{2,0},{3,1},{4,6},{5,7},{6,4},{7,5},{8,10},{9,11},{10,... | collective-permute-start | bytes 294920 | tf_op jit(solution)/shard_map/ppermute | solution.py:248
  103.7 11.2 %collective-permute-start.11 = (bf16[32,1536]{1,0:T(8,128)(2,1)S(1)}, bf16[32,1536]{1,0:T(8,128)(2,1)S(1)}, u32[]{:S(2)}, u32[]{:S(2)}) collective-permute-start(bf16[32,1536]{1,0:T(8,128)(2,1)S(1)} %dynamic-slice_convert_fusion), channel_id=1, source_target_pairs={{0,2},{1,3},{2,0},{3,1},{4,6},{5,7},{6,4},{7,5},{8,10},{9,11},{10,... | collective-permute-start | bytes 294920 | tf_op jit(solution)/shard_map/ppermute | solution.py:248
  107.9 10.7 %collective-permute-start.9 = (bf16[16,1536]{1,0:T(8,128)(2,1)S(1)}, bf16[16,1536]{1,0:T(8,128)(2,1)S(1)}, u32[]{:S(2)}, u32[]{:S(2)}) collective-permute-start(bf16[16,1536]{1,0:T(8,128)(2,1)S(1)} %dynamic-slice_convert_fusion.3), channel_id=1, source_target_pairs={{0,4},{1,5},{2,6},{3,7},{4,0},{5,1},{6,2},{7,3},{8,12},{9,13},{10,... | collective-permute-start | bytes 147464 | tf_op jit(solution)/shard_map/ppermute | solution.py:248
  115.0 10.3 %collective-permute-start.12 = (bf16[16,1536]{1,0:T(8,128)(2,1)S(1)}, bf16[16,1536]{1,0:T(8,128)(2,1)S(1)}, u32[]{:S(2)}, u32[]{:S(2)}) collective-permute-start(bf16[16,1536]{1,0:T(8,128)(2,1)S(1)} %dynamic-slice_convert_fusion.2), channel_id=1, source_target_pairs={{0,4},{1,5},{2,6},{3,7},{4,0},{5,1},{6,2},{7,3},{8,12},{9,13},{10,... | collective-permute-start | bytes 147464 | tf_op jit(solution)/shard_map/ppermute | solution.py:248

commit v4 on v3

--- a/solution.py
+++ b/solution.py
@@ -77,6 +77,11 @@
             q_ref[i, rows] = pieces_ref[piece, 0]
         for part in range(2):
             next_ref[part, rows] = pieces_ref[piece, 1 + part]
+
+
+def stage_body(block_ref, after_ref, out_ref):
+    del after_ref
+    out_ref[...] = block_ref[...]
 
 
 def after_body(block_ref, out_ref):
@@ -211,7 +216,8 @@
 
     other_z = lax.ppermute(stale_kv, "zh", swap(2, 1))
     other_z = call(after_body, shape(other_z.shape, BF16), 1, flops=LONG, name="after")(other_z)
-    here, there = ([kv] + [lax.ppermute(kv, "x", shift(4, by)) for by in (1, 3, 2)] for kv in (stale_kv, other_z))
+    here = [stale_kv] + [lax.ppermute(stale_kv, "x", shift(4, by)) for by in (1, 3)]
+    there = [other_z] + [lax.ppermute(other_z, "x", shift(4, by)) for by in (1, 3, 2)]
 
     q_spread, next_kv = call(
         unpack_body,
@@ -220,6 +226,8 @@
         in_specs=[VMEM, ANY, ANY],
         name="unpack",
     )(pieces, *here[1:3])
+    staged = call(stage_body, shape(stale_kv.shape, BF16), 2, in_specs=[VMEM, ANY], name="stage")(stale_kv, q_spread)
+    here.append(lax.ppermute(staged, "x", shift(4, 2)))
     queries = lax.all_to_all(q_spread, ("y", "core"), 0, 0, tiled=True)
 
     partial = attend(True, pos, queries, next_kv, *here)

time: 128 us -> 128 us (level)
    all_to_all x1, waiting for transfers between devices: 2.35 us -> 0.01 us  [local(): queries = lax.all_to_all(q_spread, ('y', 'core'), 0, 0, tiled=True)]
    ppermute x6, starting transfers between devices: 34.1 us -> 32 us  [local(): kept = kept + lax.ppermute(sent, 'head', swap(N_HEAD, bit)).astype(F32)]
    ppermute x6, waiting for transfers between devices: 1.37 us -> 3.42 us  [the longest x3 3.42 us: local(): lax.ppermute(other_z, 'x', shift(4, by))]
    all_to_all x1, starting transfers between devices: 6.54 us -> 8.48 us  [local(): queries = lax.all_to_all(q_spread, ('y', 'core'), 0, 0, tiled=True)]
  transfers between devices with their start and end apart: 15 -> 15, of which waited for: 4 -> 5; matrix products, arithmetic and copies ran while one was open for 0% -> 0% of each run, Pallas kernels for 3% -> 3%
where the time goes in v4:
time: 128 us; the launch traced here: 126 us
  starting transfers between devices  81 us (63%)
  blocking collectives  19 us (15%)
  waiting for transfers between devices  13.1 us (10%)
  Pallas kernels  9.76 us (8%)
    ppermute x6, starting transfers between devices, local(): kept = kept + lax.ppermute(sent, 'head', swap(N_HEAD, bit)).astype(F32)  32 us
    all_to_all x1, blocking collectives, local(): parts = lax.all_to_all(partial, ('y', 'core'), 0, 0, tiled=True)  19 us
    all_to_all x1, starting transfers between devices, local(): pieces = lax.all_to_all(packed, 'head', 0, 0, tiled=True)  13.1 us
    ppermute x6, waiting for transfers between devices, local(): kept = kept + lax.ppermute(sent, 'head', swap(N_HEAD, bit)).astype(F32)  9.09 us
    all_to_all x1, starting transfers between devices, local(): queries = lax.all_to_all(q_spread, ('y', 'core'), 0, 0, tiled=True)  8.48 us
    ppermute x3, starting transfers between devices, local(): lax.ppermute(other_z, 'x', shift(4, by))  8.43 us
    ppermute x1, starting transfers between devices, local(): other_z = lax.ppermute(stale_kv, 'zh', swap(2, 1))  7.94 us
    pallas_call x2, Pallas kernels, attend(): call(functools.partial(attend_body, own_first), shape((QUERY_SLABS, ROWS,...  6.31 us
  transfers between devices with their start and end apart: 15, of which 5 were waited for; matrix products, arithmetic and copies ran while one was open for 0% of the time, Pallas kernels for 3%

profile of v4, /device:TPU:1, one launch (start us, length us, event | category | flops | bytes accessed | tf_op | source)
XLA Modules:
  0.0 126.0 jit_solution(11777569176070141397)
XLA Ops:
  2.3 13.1 %all-to-all-start = ((bf16[8,3,16,384]{3,2,1,0:T(8,128)(2,1)}), bf16[8,3,16,384]{3,2,1,0:T(8,128)(2,1)S(1)}, u32[]{:S(2)}, u32[]{:S(2)}) async-start(bf16[8,3,16,384]{3,2,1,0:T(8,128)(2,1)} %pack.1), calls=%async_computation | async-start | bytes 589824 | tf_op jit(solution)/shard_map/all_to_all | solution.py:215
  15.4 4.4 %collective-permute-start.1 = (bf16[2,128,384]{2,1,0:T(8,128)(2,1)}, bf16[2,128,384]{2,1,0:T(8,128)(2,1)S(1)}, u32[]{:S(2)}, u32[]{:S(2)}) collective-permute-start(bf16[2,128,384]{2,1,0:T(8,128)(2,1)} %rest_0_.1), channel_id=1, source_target_pairs={{0,96},{32,0},{64,32},{96,64},{1,97},{33,1},{65,33},{97,65},{2,98}... | collective-permute-start | bytes 589832 | tf_op jit(solution)/shard_map/ppermute | solution.py:219
  19.8 1.9 %collective-permute-start = (bf16[2,128,384]{2,1,0:T(8,128)(2,1)}, bf16[2,128,384]{2,1,0:T(8,128)(2,1)S(1)}, u32[]{:S(2)}, u32[]{:S(2)}) collective-permute-start(bf16[2,128,384]{2,1,0:T(8,128)(2,1)} %rest_0_.1), channel_id=1, source_target_pairs={{0,32},{32,64},{64,96},{96,0},{1,33},{33,65},{65,97},{97,1},{2,34}... | collective-permute-start | bytes 589832 | tf_op jit(solution)/shard_map/ppermute | solution.py:219
  21.7 7.9 %collective-permute-start.3 = (bf16[2,128,384]{2,1,0:T(8,128)(2,1)}, bf16[2,128,384]{2,1,0:T(8,128)(2,1)S(1)}, u32[]{:S(2)}, u32[]{:S(2)}) collective-permute-start(bf16[2,128,384]{2,1,0:T(8,128)(2,1)} %rest_0_.1), channel_id=1, source_target_pairs={{0,16},{16,0},{1,17},{17,1},{2,18},{18,2},{3,19},{19,3},{4,20},{20... | collective-permute-start | bytes 589832 | tf_op jit(solution)/shard_map/ppermute | solution.py:217
  30.3 1.0 unpack.1
  31.3 8.5 %all-to-all-start.1 = ((bf16[8,128,384]{2,1,0:T(8,128)(2,1)}), bf16[8,128,384]{2,1,0:T(8,128)(2,1)S(1)}, u32[]{:S(2)}, u32[]{:S(2)}) async-start(bf16[8,128,384]{2,1,0:T(8,128)(2,1)} %get-tuple-element.8.after_ref), calls=%async_computation.1 | async-start | bytes 1572864 | tf_op jit(solution)/shard_map/all_to_all | solution.py:231
  39.9 4.8 %collective-permute-start.2 = (bf16[2,128,384]{2,1,0:T(8,128)(2,1)S(1)}, bf16[2,128,384]{2,1,0:T(8,128)(2,1)S(1)}, u32[]{:S(2)}, u32[]{:S(2)}) collective-permute-start(bf16[2,128,384]{2,1,0:T(8,128)(2,1)S(1)} %stage.1), channel_id=1, source_target_pairs={{0,64},{32,96},{64,0},{96,32},{1,65},{33,97},{65,1},{97,33},{2,66}... | collective-permute-start | bytes 589832 | tf_op jit(solution)/shard_map/ppermute | solution.py:230
  44.7 2.1 %collective-permute-start.6 = (bf16[2,128,384]{2,1,0:T(8,128)(2,1)S(1)}, bf16[2,128,384]{2,1,0:T(8,128)(2,1)S(1)}, u32[]{:S(2)}, u32[]{:S(2)}) collective-permute-start(bf16[2,128,384]{2,1,0:T(8,128)(2,1)S(1)} %after.1.rest_0_), channel_id=1, source_target_pairs={{0,64},{32,96},{64,0},{96,32},{1,65},{33,97},{65,1},{97,33},{2,66}... | collective-permute-start | bytes 589832 | tf_op jit(solution)/shard_map/ppermute | solution.py:220
  46.8 4.4 %collective-permute-start.5 = (bf16[2,128,384]{2,1,0:T(8,128)(2,1)S(1)}, bf16[2,128,384]{2,1,0:T(8,128)(2,1)S(1)}, u32[]{:S(2)}, u32[]{:S(2)}) collective-permute-start(bf16[2,128,384]{2,1,0:T(8,128)(2,1)S(1)} %after.1.rest_0_), channel_id=1, source_target_pairs={{0,96},{32,0},{64,32},{96,64},{1,97},{33,1},{65,33},{97,65},{2,98}... | collective-permute-start | bytes 589832 | tf_op jit(solution)/shard_map/ppermute | solution.py:220
  51.2 1.9 %collective-permute-start.4 = (bf16[2,128,384]{2,1,0:T(8,128)(2,1)S(1)}, bf16[2,128,384]{2,1,0:T(8,128)(2,1)S(1)}, u32[]{:S(2)}, u32[]{:S(2)}) collective-permute-start(bf16[2,128,384]{2,1,0:T(8,128)(2,1)S(1)} %after.1.rest_0_), channel_id=1, source_target_pairs={{0,32},{32,64},{64,96},{96,0},{1,33},{33,65},{65,97},{97,1},{2,34}... | collective-permute-start | bytes 589832 | tf_op jit(solution)/shard_map/ppermute | solution.py:220
  53.3 3.2 %attend.2.other_ref = bf16[8,400,128]{2,1,0:T(8,128)(2,1)S(1)} custom-call(s32[3]{0:T(128)S(1)} %pad_add_fusion.pos_ref, bf16[8,128,384]{2,1,0:T(8,128)(2,1)S(1)} %all-to-all-done.1.q_ref, bf16[2,128,384]{2,1,0:T(8,128)(2,1)S(1)} %copy-done.3, bf16[2,128,384]{2,1,0:T(8,128)(2,1)S(1)} %copy-done.2, ...), custom_call_target="tpu_custom_call" | custom-call | flops 805306368 | bytes 524288 | tf_op jit(solution)/shard_map/attend/pallas_call | solution.py:176
  56.5 1.9 %collective-permute-done.5.rest_2_ = bf16[2,128,384]{2,1,0:T(8,128)(2,1)S(1)} collective-permute-done((bf16[2,128,384]{2,1,0:T(8,128)(2,1)S(1)}, bf16[2,128,384]{2,1,0:T(8,128)(2,1)S(1)}, u32[]{:S(2)}, u32[]{:S(2)}) %collective-permute-start.5) | collective-permute-done | bytes 196640 | tf_op jit(solution)/shard_map/ppermute | solution.py:220
  58.4 1.5 %collective-permute-done.4.rest_1_ = bf16[2,128,384]{2,1,0:T(8,128)(2,1)S(1)} collective-permute-done((bf16[2,128,384]{2,1,0:T(8,128)(2,1)S(1)}, bf16[2,128,384]{2,1,0:T(8,128)(2,1)S(1)}, u32[]{:S(2)}, u32[]{:S(2)}) %collective-permute-start.4) | collective-permute-done | bytes 196640 | tf_op jit(solution)/shard_map/ppermute | solution.py:220
  59.9 3.1 %attend.3 = bf16[8,400,128]{2,1,0:T(8,128)(2,1)S(1)} custom-call(s32[3]{0:T(128)S(1)} %pad_add_fusion.pos_ref, bf16[8,128,384]{2,1,0:T(8,128)(2,1)S(1)} %all-to-all-done.1.q_ref, bf16[8,400,128]{2,1,0:T(8,128)(2,1)S(1)} %attend.2.other_ref, bf16[2,128,384]{2,1,0:T(8,128)(2,1)S(1)} %after.1.rest_0_, bf16[2,128,384]{2,1,0:T(8,128)(2,1)S(1)} %collective-permute-done.4.rest_1_, ...), custom_call_target="tpu_custom_call" | custom-call | flops 805306368 | bytes 524288 | tf_op jit(solution)/shard_map/attend/pallas_call | solution.py:176
  63.0 19.0 %all_to_all.15.parts_ref = bf16[8,400,128]{2,1,0:T(8,128)(2,1)S(1)} all-to-all(bf16[8,400,128]{2,1,0:T(8,128)(2,1)S(1)} %attend.3), channel_id=1, replica_groups=mesh['y'=4,'x'=4,'zh'=2,'core'=2,'head'=8] {'y','core'}, dimensions={0} | all-to-all | bytes 1638400 | tf_op jit(solution)/shard_map/all_to_all | solution.py:235
  82.0 1.7 %project.1 = (f32[64,1536]{1,0:T(8,128)S(1)}, bf16[64,1536]{1,0:T(8,128)(2,1)S(1)}, f32[64,1536]{1,0:T(8,128)S(1)}, bf16[64,1536]{1,0:T(8,128)(2,1)S(1)}) custom-call(s32[3]{0:T(128)S(1)} %pad_add_fusion.pos_ref, bf16[8,400,128]{2,1,0:T(8,128)(2,1)S(1)} %all_to_all.15.parts_ref, bf16[384,3072]{1,0:T(8,128)(2,1)S(1)} %copy-done), custom_call_target="tpu_custom_call" | custom-call | bytes 524288 | tf_op jit(solution)/shard_map/project/pallas_call | solution.py:238
  83.7 3.4 %collective-permute-start.7 = (bf16[64,1536]{1,0:T(8,128)(2,1)S(1)}, bf16[64,1536]{1,0:T(8,128)(2,1)S(1)}, u32[]{:S(2)}, u32[]{:S(2)}) collective-permute-start(bf16[64,1536]{1,0:T(8,128)(2,1)S(1)} %get-tuple-element.11), channel_id=1, source_target_pairs={{0,1},{1,0},{2,3},{3,2},{4,5},{5,4},{6,7},{7,6},{8,9},{9,8},{10,11... | collective-permute-start | bytes 589832 | tf_op jit(solution)/shard_map/ppermute | solution.py:256
  87.2 2.0 %collective-permute-start.10 = (bf16[64,1536]{1,0:T(8,128)(2,1)S(1)}, bf16[64,1536]{1,0:T(8,128)(2,1)S(1)}, u32[]{:S(2)}, u32[]{:S(2)}) collective-permute-start(bf16[64,1536]{1,0:T(8,128)(2,1)S(1)} %get-tuple-element.13), channel_id=1, source_target_pairs={{0,1},{1,0},{2,3},{3,2},{4,5},{5,4},{6,7},{7,6},{8,9},{9,8},{10,11... | collective-permute-start | bytes 589832 | tf_op jit(solution)/shard_map/ppermute | solution.py:256
  89.2 2.4 %collective-permute-done.7 = bf16[64,1536]{1,0:T(8,128)(2,1)S(1)} collective-permute-done((bf16[64,1536]{1,0:T(8,128)(2,1)S(1)}, bf16[64,1536]{1,0:T(8,128)(2,1)S(1)}, u32[]{:S(2)}, u32[]{:S(2)}) %collective-permute-start.7) | collective-permute-done | bytes 196640 | tf_op jit(solution)/shard_map/ppermute | solution.py:256
  91.7 11.9 %collective-permute-start.8 = (bf16[32,1536]{1,0:T(8,128)(2,1)S(1)}, bf16[32,1536]{1,0:T(8,128)(2,1)S(1)}, u32[]{:S(2)}, u32[]{:S(2)}) collective-permute-start(bf16[32,1536]{1,0:T(8,128)(2,1)S(1)} %dynamic-slice_convert_fusion.1), channel_id=1, source_target_pairs={{0,2},{1,3},{2,0},{3,1},{4,6},{5,7},{6,4},{7,5},{8,10},{9,11},{10,... | collective-permute-start | bytes 294920 | tf_op jit(solution)/shard_map/ppermute | solution.py:256
  103.7 4.1 %collective-permute-start.11 = (bf16[32,1536]{1,0:T(8,128)(2,1)S(1)}, bf16[32,1536]{1,0:T(8,128)(2,1)S(1)}, u32[]{:S(2)}, u32[]{:S(2)}) collective-permute-start(bf16[32,1536]{1,0:T(8,128)(2,1)S(1)} %dynamic-slice_convert_fusion), channel_id=1, source_target_pairs={{0,2},{1,3},{2,0},{3,1},{4,6},{5,7},{6,4},{7,5},{8,10},{9,11},{10,... | collective-permute-start | bytes 294920 | tf_op jit(solution)/shard_map/ppermute | solution.py:256
  107.9 7.0 %collective-permute-start.9 = (bf16[16,1536]{1,0:T(8,128)(2,1)S(1)}, bf16[16,1536]{1,0:T(8,128)(2,1)S(1)}, u32[]{:S(2)}, u32[]{:S(2)}) collective-permute-start(bf16[16,1536]{1,0:T(8,128)(2,1)S(1)} %dynamic-slice_convert_fusion.3), channel_id=1, source_target_pairs={{0,4},{1,5},{2,6},{3,7},{4,0},{5,1},{6,2},{7,3},{8,12},{9,13},{10,... | collective-permute-start | bytes 147464 | tf_op jit(solution)/shard_map/ppermute | solution.py:256
  115.0 3.5 %collective-permute-start.12 = (bf16[16,1536]{1,0:T(8,128)(2,1)S(1)}, bf16[16,1536]{1,0:T(8,128)(2,1)S(1)}, u32[]{:S(2)}, u32[]{:S(2)}) collective-permute-start(bf16[16,1536]{1,0:T(8,128)(2,1)S(1)} %dynamic-slice_convert_fusion.2), channel_id=1, source_target_pairs={{0,4},{1,5},{2,6},{3,7},{4,0},{5,1},{6,2},{7,3},{8,12},{9,13},{10,... | collective-permute-start | bytes 147464 | tf_op jit(solution)/shard_map/ppermute | solution.py:256
  118.6 6.7 %collective-permute-done.12 = bf16[16,1536]{1,0:T(8,128)(2,1)S(1)} collective-permute-done((bf16[16,1536]{1,0:T(8,128)(2,1)S(1)}, bf16[16,1536]{1,0:T(8,128)(2,1)S(1)}, u32[]{:S(2)}, u32[]{:S(2)}) %collective-permute-start.12) | collective-permute-done | bytes 49184 | tf_op jit(solution)/shard_map/ppermute | solution.py:256
  (38 shorter events, 3.4 us)
Async XLA Ops:
  0.6 1.0 copy-start.1
  1.6 38.2 %copy-start.2 = (bf16[2,128,384]{2,1,0:T(8,128)(2,1)S(1)}, bf16[2,128,384]{2,1,0:T(8,128)(2,1)}, u32[]{:S(2)}) copy-start(bf16[2,128,384]{2,1,0:T(8,128)(2,1)} %rest_0_.1) | copy-start | bytes 589828
  2.3 28.0 %all-to-all-start = ((bf16[8,3,16,384]{3,2,1,0:T(8,128)(2,1)}), bf16[8,3,16,384]{3,2,1,0:T(8,128)(2,1)S(1)}, u32[]{:S(2)}, u32[]{:S(2)}) async-start(bf16[8,3,16,384]{3,2,1,0:T(8,128)(2,1)} %pack.1), calls=%async_computation | async-start | bytes 589824 | tf_op jit(solution)/shard_map/all_to_all | solution.py:215
  15.4 14.3 %collective-permute-start.1 = (bf16[2,128,384]{2,1,0:T(8,128)(2,1)}, bf16[2,128,384]{2,1,0:T(8,128)(2,1)S(1)}, u32[]{:S(2)}, u32[]{:S(2)}) collective-permute-start(bf16[2,128,384]{2,1,0:T(8,128)(2,1)} %rest_0_.1), channel_id=1, source_target_pairs={{0,96},{32,0},{64,32},{96,64},{1,97},{33,1},{65,33},{97,65},{2,98}... | collective-permute-start | bytes 589832 | tf_op jit(solution)/shard_map/ppermute | solution.py:219
  19.8 9.9 %collective-permute-start = (bf16[2,128,384]{2,1,0:T(8,128)(2,1)}, bf16[2,128,384]{2,1,0:T(8,128)(2,1)S(1)}, u32[]{:S(2)}, u32[]{:S(2)}) collective-permute-start(bf16[2,128,384]{2,1,0:T(8,128)(2,1)} %rest_0_.1), channel_id=1, source_target_pairs={{0,32},{32,64},{64,96},{96,0},{1,33},{33,65},{65,97},{97,1},{2,34}... | collective-permute-start | bytes 589832 | tf_op jit(solution)/shard_map/ppermute | solution.py:219
  21.7 22.9 %collective-permute-start.3 = (bf16[2,128,384]{2,1,0:T(8,128)(2,1)}, bf16[2,128,384]{2,1,0:T(8,128)(2,1)S(1)}, u32[]{:S(2)}, u32[]{:S(2)}) collective-permute-start(bf16[2,128,384]{2,1,0:T(8,128)(2,1)} %rest_0_.1), channel_id=1, source_target_pairs={{0,16},{16,0},{1,17},{17,1},{2,18},{18,2},{3,19},{19,3},{4,20},{20... | collective-permute-start | bytes 589832 | tf_op jit(solution)/shard_map/ppermute | solution.py:217
  31.3 21.9 %all-to-all-start.1 = ((bf16[8,128,384]{2,1,0:T(8,128)(2,1)}), bf16[8,128,384]{2,1,0:T(8,128)(2,1)S(1)}, u32[]{:S(2)}, u32[]{:S(2)}) async-start(bf16[8,128,384]{2,1,0:T(8,128)(2,1)} %get-tuple-element.8.after_ref), calls=%async_computation.1 | async-start | bytes 1572864 | tf_op jit(solution)/shard_map/all_to_all | solution.py:231
  39.8 13.4 %copy-start.3 = (bf16[2,128,384]{2,1,0:T(8,128)(2,1)S(1)}, bf16[2,128,384]{2,1,0:T(8,128)(2,1)}, u32[]{:S(2)}) copy-start(bf16[2,128,384]{2,1,0:T(8,128)(2,1)} %get-tuple-element.7.other_ref) | copy-start | bytes 589828
  39.9 13.4 %collective-permute-start.2 = (bf16[2,128,384]{2,1,0:T(8,128)(2,1)S(1)}, bf16[2,128,384]{2,1,0:T(8,128)(2,1)S(1)}, u32[]{:S(2)}, u32[]{:S(2)}) collective-permute-start(bf16[2,128,384]{2,1,0:T(8,128)(2,1)S(1)} %stage.1), channel_id=1, source_target_pairs={{0,64},{32,96},{64,0},{96,32},{1,65},{33,97},{65,1},{97,33},{2,66}... | collective-permute-start | bytes 589832 | tf_op jit(solution)/shard_map/ppermute | solution.py:230
  44.7 11.8 %collective-permute-start.6 = (bf16[2,128,384]{2,1,0:T(8,128)(2,1)S(1)}, bf16[2,128,384]{2,1,0:T(8,128)(2,1)S(1)}, u32[]{:S(2)}, u32[]{:S(2)}) collective-permute-start(bf16[2,128,384]{2,1,0:T(8,128)(2,1)S(1)} %after.1.rest_0_), channel_id=1, source_target_pairs={{0,64},{32,96},{64,0},{96,32},{1,65},{33,97},{65,1},{97,33},{2,66}... | collective-permute-start | bytes 589832 | tf_op jit(solution)/shard_map/ppermute | solution.py:220
  46.8 11.6 %collective-permute-start.5 = (bf16[2,128,384]{2,1,0:T(8,128)(2,1)S(1)}, bf16[2,128,384]{2,1,0:T(8,128)(2,1)S(1)}, u32[]{:S(2)}, u32[]{:S(2)}) collective-permute-start(bf16[2,128,384]{2,1,0:T(8,128)(2,1)S(1)} %after.1.rest_0_), channel_id=1, source_target_pairs={{0,96},{32,0},{64,32},{96,64},{1,97},{33,1},{65,33},{97,65},{2,98}... | collective-permute-start | bytes 589832 | tf_op jit(solution)/shard_map/ppermute | solution.py:220
  51.2 8.7 %collective-permute-start.4 = (bf16[2,128,384]{2,1,0:T(8,128)(2,1)S(1)}, bf16[2,128,384]{2,1,0:T(8,128)(2,1)S(1)}, u32[]{:S(2)}, u32[]{:S(2)}) collective-permute-start(bf16[2,128,384]{2,1,0:T(8,128)(2,1)S(1)} %after.1.rest_0_), channel_id=1, source_target_pairs={{0,32},{32,64},{64,96},{96,0},{1,33},{33,65},{65,97},{97,1},{2,34}... | collective-permute-start | bytes 589832 | tf_op jit(solution)/shard_map/ppermute | solution.py:220
  56.4 25.6 %copy-start = (bf16[384,3072]{1,0:T(8,128)(2,1)S(1)}, bf16[384,3072]{1,0:T(8,128)(2,1)}, u32[]{:S(2)}) copy-start(bf16[384,3072]{1,0:T(8,128)(2,1)} %w_hbm.1) | copy-start | bytes 7077892
  83.7 41.6 %copy-start.4 = (bf16[16,3072]{1,0:T(8,128)(2,1)S(1)}, bf16[16,3072]{1,0:T(8,128)(2,1)}, u32[]{:S(2)}) copy-start(bf16[16,3072]{1,0:T(8,128)(2,1)} %param.9) | copy-start | bytes 294916
  83.7 41.6 %copy-start.5 = (f32[3072]{0:T(1024)S(1)}, f32[3072]{0:T(1024)}, u32[]{:S(2)}) copy-start(f32[3072]{0:T(1024)} %param.8) | copy-start | bytes 36868
  83.7 7.9 %collective-permute-start.7 = (bf16[64,1536]{1,0:T(8,128)(2,1)S(1)}, bf16[64,1536]{1,0:T(8,128)(2,1)S(1)}, u32[]{:S(2)}, u32[]{:S(2)}) collective-permute-start(bf16[64,1536]{1,0:T(8,128)(2,1)S(1)} %get-tuple-element.11), channel_id=1, source_target_pairs={{0,1},{1,0},{2,3},{3,2},{4,5},{5,4},{6,7},{7,6},{8,9},{9,8},{10,11... | collective-permute-start | bytes 589832 | tf_op jit(solution)/shard_map/ppermute | solution.py:256
  87.2 16.4 %collective-permute-start.10 = (bf16[64,1536]{1,0:T(8,128)(2,1)S(1)}, bf16[64,1536]{1,0:T(8,128)(2,1)S(1)}, u32[]{:S(2)}, u32[]{:S(2)}) collective-permute-start(bf16[64,1536]{1,0:T(8,128)(2,1)S(1)} %get-tuple-element.13), channel_id=1, source_target_pairs={{0,1},{1,0},{2,3},{3,2},{4,5},{5,4},{6,7},{7,6},{8,9},{9,8},{10,11... | collective-permute-start | bytes 589832 | tf_op jit(solution)/shard_map/ppermute | solution.py:256
  91.7 16.1 %collective-permute-start.8 = (bf16[32,1536]{1,0:T(8,128)(2,1)S(1)}, bf16[32,1536]{1,0:T(8,128)(2,1)S(1)}, u32[]{:S(2)}, u32[]{:S(2)}) collective-permute-start(bf16[32,1536]{1,0:T(8,128)(2,1)S(1)} %dynamic-slice_convert_fusion.1), channel_id=1, source_target_pairs={{0,2},{1,3},{2,0},{3,1},{4,6},{5,7},{6,4},{7,5},{8,10},{9,11},{10,... | collective-permute-start | bytes 294920 | tf_op jit(solution)/shard_map/ppermute | solution.py:256
  103.7 11.2 %collective-permute-start.11 = (bf16[32,1536]{1,0:T(8,128)(2,1)S(1)}, bf16[32,1536]{1,0:T(8,128)(2,1)S(1)}, u32[]{:S(2)}, u32[]{:S(2)}) collective-permute-start(bf16[32,1536]{1,0:T(8,128)(2,1)S(1)} %dynamic-slice_convert_fusion), channel_id=1, source_target_pairs={{0,2},{1,3},{2,0},{3,1},{4,6},{5,7},{6,4},{7,5},{8,10},{9,11},{10,... | collective-permute-start | bytes 294920 | tf_op jit(solution)/shard_map/ppermute | solution.py:256
  107.9 10.6 %collective-permute-start.9 = (bf16[16,1536]{1,0:T(8,128)(2,1)S(1)}, bf16[16,1536]{1,0:T(8,128)(2,1)S(1)}, u32[]{:S(2)}, u32[]{:S(2)}) collective-permute-start(bf16[16,1536]{1,0:T(8,128)(2,1)S(1)} %dynamic-slice_convert_fusion.3), channel_id=1, source_target_pairs={{0,4},{1,5},{2,6},{3,7},{4,0},{5,1},{6,2},{7,3},{8,12},{9,13},{10,... | collective-permute-start | bytes 147464 | tf_op jit(solution)/shard_map/ppermute | solution.py:256
  115.0 10.2 %collective-permute-start.12 = (bf16[16,1536]{1,0:T(8,128)(2,1)S(1)}, bf16[16,1536]{1,0:T(8,128)(2,1)S(1)}, u32[]{:S(2)}, u32[]{:S(2)}) collective-permute-start(bf16[16,1536]{1,0:T(8,128)(2,1)S(1)} %dynamic-slice_convert_fusion.2), channel_id=1, source_target_pairs={{0,4},{1,5},{2,6},{3,7},{4,0},{5,1},{6,2},{7,3},{8,12},{9,13},{10,... | collective-permute-start | bytes 147464 | tf_op jit(solution)/shard_map/ppermute | solution.py:256

commit v5 on v4

--- a/solution.py
+++ b/solution.py
@@ -21,7 +21,7 @@
 KEY_SLABS = 4
 KEYS = KEY_SLABS * SLAB
 QUERY_SLABS = 8
-PARTS = 2
+PART_COLUMNS = (1792, 1280)
 LONG = 40_000_000_000
 STAT_ROWS = 16
 ROWS = WIDTH + STAT_ROWS
@@ -202,7 +202,8 @@
     mine = pl.ds(pl.multiple_of(bit * half, half), half)
     theirs = pl.ds(pl.multiple_of((1 - bit) * half, half), half)
     for part, (keep_out, send_out) in enumerate(zip(outs[0::2], outs[1::2])):
-        cols = slice(part * D // PARTS, (part + 1) * D // PARTS)
+        first = sum(PART_COLUMNS[:part])
+        cols = slice(first, first + PART_COLUMNS[part])
         keep_out[...] = proj_ref[mine, cols]
         send_out[...] = proj_ref[theirs, cols].astype(BF16)
 
@@ -234,10 +235,9 @@
     partial = attend(False, pos, queries, partial, *there)
     parts = lax.all_to_all(partial, ("y", "core"), 0, 0, tiled=True)
 
-    half = (SLAB // 2, D // PARTS)
     parts = call(
         project_body,
-        (shape(half, F32), shape(half, BF16)) * PARTS,
+        tuple(shape((SLAB // 2, n), dtype) for n in PART_COLUMNS for dtype in (F32, BF16)),
         3,
         scratch=[
             pltpu.VMEM((SLAB, WIDTH), BF16),

time: 128 us -> 128 us (level)
  waiting for transfers between devices: 13.1 us -> 10.4 us
  starting transfers between devices: 81 us -> 83.6 us
    ppermute x6, waiting for transfers between devices: 9.09 us -> 6.38 us  [local(): kept = kept + lax.ppermute(sent, 'head', swap(N_HEAD, bit)).astype(F32)]
    ppermute x6, starting transfers between devices: 32 us -> 34.6 us  [local(): kept = kept + lax.ppermute(sent, 'head', swap(N_HEAD, bit)).astype(F32)]
where the time goes in v5:
time: 128 us; the launch traced here: 126 us
  starting transfers between devices  83.6 us (65%)
  blocking collectives  19 us (15%)
  waiting for transfers between devices  10.4 us (8%)
  Pallas kernels  9.76 us (8%)
    ppermute x6, starting transfers between devices, local(): kept = kept + lax.ppermute(sent, 'head', swap(N_HEAD, bit)).astype(F32)  34.6 us
    all_to_all x1, blocking collectives, local(): parts = lax.all_to_all(partial, ('y', 'core'), 0, 0, tiled=True)  19 us
    all_to_all x1, starting transfers between devices, local(): pieces = lax.all_to_all(packed, 'head', 0, 0, tiled=True)  13.1 us
    all_to_all x1, starting transfers between devices, local(): queries = lax.all_to_all(q_spread, ('y', 'core'), 0, 0, tiled=True)  8.48 us
    ppermute x3, starting transfers between devices, local(): lax.ppermute(other_z, 'x', shift(4, by))  8.43 us
    ppermute x1, starting transfers between devices, local(): other_z = lax.ppermute(stale_kv, 'zh', swap(2, 1))  7.94 us
    ppermute x6, waiting for transfers between devices, local(): kept = kept + lax.ppermute(sent, 'head', swap(N_HEAD, bit)).astype(F32)  6.38 us
    pallas_call x2, Pallas kernels, attend(): call(functools.partial(attend_body, own_first), shape((QUERY_SLABS, ROWS,...  6.31 us
  transfers between devices with their start and end apart: 15, of which 5 were waited for; matrix products, arithmetic and copies ran while one was open for 0% of the time, Pallas kernels for 3%

profile of v5, /device:TPU:1, one launch (start us, length us, event | category | flops | bytes accessed | tf_op | source)
XLA Modules:
  0.0 125.9 jit_solution(16050409568148424848)
XLA Ops:
  2.3 13.1 %all-to-all-start = ((bf16[8,3,16,384]{3,2,1,0:T(8,128)(2,1)}), bf16[8,3,16,384]{3,2,1,0:T(8,128)(2,1)S(1)}, u32[]{:S(2)}, u32[]{:S(2)}) async-start(bf16[8,3,16,384]{3,2,1,0:T(8,128)(2,1)} %pack.1), calls=%async_computation | async-start | bytes 589824 | tf_op jit(solution)/shard_map/all_to_all | solution.py:216
  15.4 4.4 %collective-permute-start.1 = (bf16[2,128,384]{2,1,0:T(8,128)(2,1)}, bf16[2,128,384]{2,1,0:T(8,128)(2,1)S(1)}, u32[]{:S(2)}, u32[]{:S(2)}) collective-permute-start(bf16[2,128,384]{2,1,0:T(8,128)(2,1)} %rest_0_.1), channel_id=1, source_target_pairs={{0,96},{32,0},{64,32},{96,64},{1,97},{33,1},{65,33},{97,65},{2,98}... | collective-permute-start | bytes 589832 | tf_op jit(solution)/shard_map/ppermute | solution.py:220
  19.8 1.9 %collective-permute-start = (bf16[2,128,384]{2,1,0:T(8,128)(2,1)}, bf16[2,128,384]{2,1,0:T(8,128)(2,1)S(1)}, u32[]{:S(2)}, u32[]{:S(2)}) collective-permute-start(bf16[2,128,384]{2,1,0:T(8,128)(2,1)} %rest_0_.1), channel_id=1, source_target_pairs={{0,32},{32,64},{64,96},{96,0},{1,33},{33,65},{65,97},{97,1},{2,34}... | collective-permute-start | bytes 589832 | tf_op jit(solution)/shard_map/ppermute | solution.py:220
  21.7 7.9 %collective-permute-start.3 = (bf16[2,128,384]{2,1,0:T(8,128)(2,1)}, bf16[2,128,384]{2,1,0:T(8,128)(2,1)S(1)}, u32[]{:S(2)}, u32[]{:S(2)}) collective-permute-start(bf16[2,128,384]{2,1,0:T(8,128)(2,1)} %rest_0_.1), channel_id=1, source_target_pairs={{0,16},{16,0},{1,17},{17,1},{2,18},{18,2},{3,19},{19,3},{4,20},{20... | collective-permute-start | bytes 589832 | tf_op jit(solution)/shard_map/ppermute | solution.py:218
  30.3 1.0 unpack.1
  31.3 8.5 %all-to-all-start.1 = ((bf16[8,128,384]{2,1,0:T(8,128)(2,1)}), bf16[8,128,384]{2,1,0:T(8,128)(2,1)S(1)}, u32[]{:S(2)}, u32[]{:S(2)}) async-start(bf16[8,128,384]{2,1,0:T(8,128)(2,1)} %get-tuple-element.8.after_ref), calls=%async_computation.1 | async-start | bytes 1572864 | tf_op jit(solution)/shard_map/all_to_all | solution.py:232
  39.9 4.8 %collective-permute-start.2 = (bf16[2,128,384]{2,1,0:T(8,128)(2,1)S(1)}, bf16[2,128,384]{2,1,0:T(8,128)(2,1)S(1)}, u32[]{:S(2)}, u32[]{:S(2)}) collective-permute-start(bf16[2,128,384]{2,1,0:T(8,128)(2,1)S(1)} %stage.1), channel_id=1, source_target_pairs={{0,64},{32,96},{64,0},{96,32},{1,65},{33,97},{65,1},{97,33},{2,66}... | collective-permute-start | bytes 589832 | tf_op jit(solution)/shard_map/ppermute | solution.py:231
  44.7 2.1 %collective-permute-start.6 = (bf16[2,128,384]{2,1,0:T(8,128)(2,1)S(1)}, bf16[2,128,384]{2,1,0:T(8,128)(2,1)S(1)}, u32[]{:S(2)}, u32[]{:S(2)}) collective-permute-start(bf16[2,128,384]{2,1,0:T(8,128)(2,1)S(1)} %after.1.rest_0_), channel_id=1, source_target_pairs={{0,64},{32,96},{64,0},{96,32},{1,65},{33,97},{65,1},{97,33},{2,66}... | collective-permute-start | bytes 589832 | tf_op jit(solution)/shard_map/ppermute | solution.py:221
  46.8 4.4 %collective-permute-start.5 = (bf16[2,128,384]{2,1,0:T(8,128)(2,1)S(1)}, bf16[2,128,384]{2,1,0:T(8,128)(2,1)S(1)}, u32[]{:S(2)}, u32[]{:S(2)}) collective-permute-start(bf16[2,128,384]{2,1,0:T(8,128)(2,1)S(1)} %after.1.rest_0_), channel_id=1, source_target_pairs={{0,96},{32,0},{64,32},{96,64},{1,97},{33,1},{65,33},{97,65},{2,98}... | collective-permute-start | bytes 589832 | tf_op jit(solution)/shard_map/ppermute | solution.py:221
  51.2 1.9 %collective-permute-start.4 = (bf16[2,128,384]{2,1,0:T(8,128)(2,1)S(1)}, bf16[2,128,384]{2,1,0:T(8,128)(2,1)S(1)}, u32[]{:S(2)}, u32[]{:S(2)}) collective-permute-start(bf16[2,128,384]{2,1,0:T(8,128)(2,1)S(1)} %after.1.rest_0_), channel_id=1, source_target_pairs={{0,32},{32,64},{64,96},{96,0},{1,33},{33,65},{65,97},{97,1},{2,34}... | collective-permute-start | bytes 589832 | tf_op jit(solution)/shard_map/ppermute | solution.py:221
  53.3 3.2 %attend.2.other_ref = bf16[8,400,128]{2,1,0:T(8,128)(2,1)S(1)} custom-call(s32[3]{0:T(128)S(1)} %pad_add_fusion.pos_ref, bf16[8,128,384]{2,1,0:T(8,128)(2,1)S(1)} %all-to-all-done.1.q_ref, bf16[2,128,384]{2,1,0:T(8,128)(2,1)S(1)} %copy-done.3, bf16[2,128,384]{2,1,0:T(8,128)(2,1)S(1)} %copy-done.2, ...), custom_call_target="tpu_custom_call" | custom-call | flops 805306368 | bytes 524288 | tf_op jit(solution)/shard_map/attend/pallas_call | solution.py:176
  56.5 1.9 %collective-permute-done.5.rest_2_ = bf16[2,128,384]{2,1,0:T(8,128)(2,1)S(1)} collective-permute-done((bf16[2,128,384]{2,1,0:T(8,128)(2,1)S(1)}, bf16[2,128,384]{2,1,0:T(8,128)(2,1)S(1)}, u32[]{:S(2)}, u32[]{:S(2)}) %collective-permute-start.5) | collective-permute-done | bytes 196640 | tf_op jit(solution)/shard_map/ppermute | solution.py:221
  58.4 1.5 %collective-permute-done.4.rest_1_ = bf16[2,128,384]{2,1,0:T(8,128)(2,1)S(1)} collective-permute-done((bf16[2,128,384]{2,1,0:T(8,128)(2,1)S(1)}, bf16[2,128,384]{2,1,0:T(8,128)(2,1)S(1)}, u32[]{:S(2)}, u32[]{:S(2)}) %collective-permute-start.4) | collective-permute-done | bytes 196640 | tf_op jit(solution)/shard_map/ppermute | solution.py:221
  59.9 3.1 %attend.3 = bf16[8,400,128]{2,1,0:T(8,128)(2,1)S(1)} custom-call(s32[3]{0:T(128)S(1)} %pad_add_fusion.pos_ref, bf16[8,128,384]{2,1,0:T(8,128)(2,1)S(1)} %all-to-all-done.1.q_ref, bf16[8,400,128]{2,1,0:T(8,128)(2,1)S(1)} %attend.2.other_ref, bf16[2,128,384]{2,1,0:T(8,128)(2,1)S(1)} %after.1.rest_0_, bf16[2,128,384]{2,1,0:T(8,128)(2,1)S(1)} %collective-permute-done.4.rest_1_, ...), custom_call_target="tpu_custom_call" | custom-call | flops 805306368 | bytes 524288 | tf_op jit(solution)/shard_map/attend/pallas_call | solution.py:176
  63.0 19.0 %all_to_all.15.parts_ref = bf16[8,400,128]{2,1,0:T(8,128)(2,1)S(1)} all-to-all(bf16[8,400,128]{2,1,0:T(8,128)(2,1)S(1)} %attend.3), channel_id=1, replica_groups=mesh['y'=4,'x'=4,'zh'=2,'core'=2,'head'=8] {'y','core'}, dimensions={0} | all-to-all | bytes 1638400 | tf_op jit(solution)/shard_map/all_to_all | solution.py:236
  82.0 1.7 %project.1 = (f32[64,1792]{1,0:T(8,128)S(1)}, bf16[64,1792]{1,0:T(8,128)(2,1)S(1)}, f32[64,1280]{1,0:T(8,128)S(1)}, bf16[64,1280]{1,0:T(8,128)(2,1)S(1)}) custom-call(s32[3]{0:T(128)S(1)} %pad_add_fusion.pos_ref, bf16[8,400,128]{2,1,0:T(8,128)(2,1)S(1)} %all_to_all.15.parts_ref, bf16[384,3072]{1,0:T(8,128)(2,1)S(1)} %copy-done), custom_call_target="tpu_custom_call" | custom-call | bytes 524288 | tf_op jit(solution)/shard_map/project/pallas_call | solution.py:238
  83.7 3.4 %collective-permute-start.10 = (bf16[64,1280]{1,0:T(8,128)(2,1)S(1)}, bf16[64,1280]{1,0:T(8,128)(2,1)S(1)}, u32[]{:S(2)}, u32[]{:S(2)}) collective-permute-start(bf16[64,1280]{1,0:T(8,128)(2,1)S(1)} %get-tuple-element.13), channel_id=1, source_target_pairs={{0,1},{1,0},{2,3},{3,2},{4,5},{5,4},{6,7},{7,6},{8,9},{9,8},{10,11... | collective-permute-start | bytes 491528 | tf_op jit(solution)/shard_map/ppermute | solution.py:256
  87.2 2.0 %collective-permute-start.7 = (bf16[64,1792]{1,0:T(8,128)(2,1)S(1)}, bf16[64,1792]{1,0:T(8,128)(2,1)S(1)}, u32[]{:S(2)}, u32[]{:S(2)}) collective-permute-start(bf16[64,1792]{1,0:T(8,128)(2,1)S(1)} %get-tuple-element.11), channel_id=1, source_target_pairs={{0,1},{1,0},{2,3},{3,2},{4,5},{5,4},{6,7},{7,6},{8,9},{9,8},{10,11... | collective-permute-start | bytes 688136 | tf_op jit(solution)/shard_map/ppermute | solution.py:256
  89.2 1.7 %collective-permute-done.10 = bf16[64,1280]{1,0:T(8,128)(2,1)S(1)} collective-permute-done((bf16[64,1280]{1,0:T(8,128)(2,1)S(1)}, bf16[64,1280]{1,0:T(8,128)(2,1)S(1)}, u32[]{:S(2)}, u32[]{:S(2)}) %collective-permute-start.10) | collective-permute-done | bytes 163872 | tf_op jit(solution)/shard_map/ppermute | solution.py:256
  91.0 11.9 %collective-permute-start.11 = (bf16[32,1280]{1,0:T(8,128)(2,1)S(1)}, bf16[32,1280]{1,0:T(8,128)(2,1)S(1)}, u32[]{:S(2)}, u32[]{:S(2)}) collective-permute-start(bf16[32,1280]{1,0:T(8,128)(2,1)S(1)} %dynamic-slice_convert_fusion.1), channel_id=1, source_target_pairs={{0,2},{1,3},{2,0},{3,1},{4,6},{5,7},{6,4},{7,5},{8,10},{9,11},{10,... | collective-permute-start | bytes 245768 | tf_op jit(solution)/shard_map/ppermute | solution.py:256
  103.0 4.3 %collective-permute-start.8 = (bf16[32,1792]{1,0:T(8,128)(2,1)S(1)}, bf16[32,1792]{1,0:T(8,128)(2,1)S(1)}, u32[]{:S(2)}, u32[]{:S(2)}) collective-permute-start(bf16[32,1792]{1,0:T(8,128)(2,1)S(1)} %dynamic-slice_convert_fusion), channel_id=1, source_target_pairs={{0,2},{1,3},{2,0},{3,1},{4,6},{5,7},{6,4},{7,5},{8,10},{9,11},{10,... | collective-permute-start | bytes 344072 | tf_op jit(solution)/shard_map/ppermute | solution.py:256
  107.3 7.6 %collective-permute-start.12 = (bf16[16,1280]{1,0:T(8,128)(2,1)S(1)}, bf16[16,1280]{1,0:T(8,128)(2,1)S(1)}, u32[]{:S(2)}, u32[]{:S(2)}) collective-permute-start(bf16[16,1280]{1,0:T(8,128)(2,1)S(1)} %dynamic-slice_convert_fusion.3), channel_id=1, source_target_pairs={{0,4},{1,5},{2,6},{3,7},{4,0},{5,1},{6,2},{7,3},{8,12},{9,13},{10,... | collective-permute-start | bytes 122888 | tf_op jit(solution)/shard_map/ppermute | solution.py:256
  115.0 5.5 %collective-permute-start.9 = (bf16[16,1792]{1,0:T(8,128)(2,1)S(1)}, bf16[16,1792]{1,0:T(8,128)(2,1)S(1)}, u32[]{:S(2)}, u32[]{:S(2)}) collective-permute-start(bf16[16,1792]{1,0:T(8,128)(2,1)S(1)} %dynamic-slice_convert_fusion.2), channel_id=1, source_target_pairs={{0,4},{1,5},{2,6},{3,7},{4,0},{5,1},{6,2},{7,3},{8,12},{9,13},{10,... | collective-permute-start | bytes 172040 | tf_op jit(solution)/shard_map/ppermute | solution.py:256
  120.5 4.6 %collective-permute-done.9 = bf16[16,1792]{1,0:T(8,128)(2,1)S(1)} collective-permute-done((bf16[16,1792]{1,0:T(8,128)(2,1)S(1)}, bf16[16,1792]{1,0:T(8,128)(2,1)S(1)}, u32[]{:S(2)}, u32[]{:S(2)}) %collective-permute-start.9) | collective-permute-done | bytes 57376 | tf_op jit(solution)/shard_map/ppermute | solution.py:256
  (38 shorter events, 3.4 us)
Async XLA Ops:
  0.6 1.0 copy-start.1
  1.6 38.2 %copy-start.2 = (bf16[2,128,384]{2,1,0:T(8,128)(2,1)S(1)}, bf16[2,128,384]{2,1,0:T(8,128)(2,1)}, u32[]{:S(2)}) copy-start(bf16[2,128,384]{2,1,0:T(8,128)(2,1)} %rest_0_.1) | copy-start | bytes 589828
  2.3 28.0 %all-to-all-start = ((bf16[8,3,16,384]{3,2,1,0:T(8,128)(2,1)}), bf16[8,3,16,384]{3,2,1,0:T(8,128)(2,1)S(1)}, u32[]{:S(2)}, u32[]{:S(2)}) async-start(bf16[8,3,16,384]{3,2,1,0:T(8,128)(2,1)} %pack.1), calls=%async_computation | async-start | bytes 589824 | tf_op jit(solution)/shard_map/all_to_all | solution.py:216
  15.4 14.3 %collective-permute-start.1 = (bf16[2,128,384]{2,1,0:T(8,128)(2,1)}, bf16[2,128,384]{2,1,0:T(8,128)(2,1)S(1)}, u32[]{:S(2)}, u32[]{:S(2)}) collective-permute-start(bf16[2,128,384]{2,1,0:T(8,128)(2,1)} %rest_0_.1), channel_id=1, source_target_pairs={{0,96},{32,0},{64,32},{96,64},{1,97},{33,1},{65,33},{97,65},{2,98}... | collective-permute-start | bytes 589832 | tf_op jit(solution)/shard_map/ppermute | solution.py:220
  19.8 9.9 %collective-permute-start = (bf16[2,128,384]{2,1,0:T(8,128)(2,1)}, bf16[2,128,384]{2,1,0:T(8,128)(2,1)S(1)}, u32[]{:S(2)}, u32[]{:S(2)}) collective-permute-start(bf16[2,128,384]{2,1,0:T(8,128)(2,1)} %rest_0_.1), channel_id=1, source_target_pairs={{0,32},{32,64},{64,96},{96,0},{1,33},{33,65},{65,97},{97,1},{2,34}... | collective-permute-start | bytes 589832 | tf_op jit(solution)/shard_map/ppermute | solution.py:220
  21.7 22.9 %collective-permute-start.3 = (bf16[2,128,384]{2,1,0:T(8,128)(2,1)}, bf16[2,128,384]{2,1,0:T(8,128)(2,1)S(1)}, u32[]{:S(2)}, u32[]{:S(2)}) collective-permute-start(bf16[2,128,384]{2,1,0:T(8,128)(2,1)} %rest_0_.1), channel_id=1, source_target_pairs={{0,16},{16,0},{1,17},{17,1},{2,18},{18,2},{3,19},{19,3},{4,20},{20... | collective-permute-start | bytes 589832 | tf_op jit(solution)/shard_map/ppermute | solution.py:218
  31.3 21.9 %all-to-all-start.1 = ((bf16[8,128,384]{2,1,0:T(8,128)(2,1)}), bf16[8,128,384]{2,1,0:T(8,128)(2,1)S(1)}, u32[]{:S(2)}, u32[]{:S(2)}) async-start(bf16[8,128,384]{2,1,0:T(8,128)(2,1)} %get-tuple-element.8.after_ref), calls=%async_computation.1 | async-start | bytes 1572864 | tf_op jit(solution)/shard_map/all_to_all | solution.py:232
  39.8 13.4 %copy-start.3 = (bf16[2,128,384]{2,1,0:T(8,128)(2,1)S(1)}, bf16[2,128,384]{2,1,0:T(8,128)(2,1)}, u32[]{:S(2)}) copy-start(bf16[2,128,384]{2,1,0:T(8,128)(2,1)} %get-tuple-element.7.other_ref) | copy-start | bytes 589828
  39.9 13.4 %collective-permute-start.2 = (bf16[2,128,384]{2,1,0:T(8,128)(2,1)S(1)}, bf16[2,128,384]{2,1,0:T(8,128)(2,1)S(1)}, u32[]{:S(2)}, u32[]{:S(2)}) collective-permute-start(bf16[2,128,384]{2,1,0:T(8,128)(2,1)S(1)} %stage.1), channel_id=1, source_target_pairs={{0,64},{32,96},{64,0},{96,32},{1,65},{33,97},{65,1},{97,33},{2,66}... | collective-permute-start | bytes 589832 | tf_op jit(solution)/shard_map/ppermute | solution.py:231
  44.7 11.8 %collective-permute-start.6 = (bf16[2,128,384]{2,1,0:T(8,128)(2,1)S(1)}, bf16[2,128,384]{2,1,0:T(8,128)(2,1)S(1)}, u32[]{:S(2)}, u32[]{:S(2)}) collective-permute-start(bf16[2,128,384]{2,1,0:T(8,128)(2,1)S(1)} %after.1.rest_0_), channel_id=1, source_target_pairs={{0,64},{32,96},{64,0},{96,32},{1,65},{33,97},{65,1},{97,33},{2,66}... | collective-permute-start | bytes 589832 | tf_op jit(solution)/shard_map/ppermute | solution.py:221
  46.8 11.6 %collective-permute-start.5 = (bf16[2,128,384]{2,1,0:T(8,128)(2,1)S(1)}, bf16[2,128,384]{2,1,0:T(8,128)(2,1)S(1)}, u32[]{:S(2)}, u32[]{:S(2)}) collective-permute-start(bf16[2,128,384]{2,1,0:T(8,128)(2,1)S(1)} %after.1.rest_0_), channel_id=1, source_target_pairs={{0,96},{32,0},{64,32},{96,64},{1,97},{33,1},{65,33},{97,65},{2,98}... | collective-permute-start | bytes 589832 | tf_op jit(solution)/shard_map/ppermute | solution.py:221
  51.2 8.7 %collective-permute-start.4 = (bf16[2,128,384]{2,1,0:T(8,128)(2,1)S(1)}, bf16[2,128,384]{2,1,0:T(8,128)(2,1)S(1)}, u32[]{:S(2)}, u32[]{:S(2)}) collective-permute-start(bf16[2,128,384]{2,1,0:T(8,128)(2,1)S(1)} %after.1.rest_0_), channel_id=1, source_target_pairs={{0,32},{32,64},{64,96},{96,0},{1,33},{33,65},{65,97},{97,1},{2,34}... | collective-permute-start | bytes 589832 | tf_op jit(solution)/shard_map/ppermute | solution.py:221
  56.4 25.6 %copy-start = (bf16[384,3072]{1,0:T(8,128)(2,1)S(1)}, bf16[384,3072]{1,0:T(8,128)(2,1)}, u32[]{:S(2)}) copy-start(bf16[384,3072]{1,0:T(8,128)(2,1)} %w_hbm.1) | copy-start | bytes 7077892
  83.7 41.5 %copy-start.4 = (bf16[16,3072]{1,0:T(8,128)(2,1)S(1)}, bf16[16,3072]{1,0:T(8,128)(2,1)}, u32[]{:S(2)}) copy-start(bf16[16,3072]{1,0:T(8,128)(2,1)} %param.9) | copy-start | bytes 294916
  83.7 41.5 %copy-start.5 = (f32[3072]{0:T(1024)S(1)}, f32[3072]{0:T(1024)}, u32[]{:S(2)}) copy-start(f32[3072]{0:T(1024)} %param.8) | copy-start | bytes 36868
  83.7 7.2 %collective-permute-start.10 = (bf16[64,1280]{1,0:T(8,128)(2,1)S(1)}, bf16[64,1280]{1,0:T(8,128)(2,1)S(1)}, u32[]{:S(2)}, u32[]{:S(2)}) collective-permute-start(bf16[64,1280]{1,0:T(8,128)(2,1)S(1)} %get-tuple-element.13), channel_id=1, source_target_pairs={{0,1},{1,0},{2,3},{3,2},{4,5},{5,4},{6,7},{7,6},{8,9},{9,8},{10,11... | collective-permute-start | bytes 491528 | tf_op jit(solution)/shard_map/ppermute | solution.py:256
  87.2 15.7 %collective-permute-start.7 = (bf16[64,1792]{1,0:T(8,128)(2,1)S(1)}, bf16[64,1792]{1,0:T(8,128)(2,1)S(1)}, u32[]{:S(2)}, u32[]{:S(2)}) collective-permute-start(bf16[64,1792]{1,0:T(8,128)(2,1)S(1)} %get-tuple-element.11), channel_id=1, source_target_pairs={{0,1},{1,0},{2,3},{3,2},{4,5},{5,4},{6,7},{7,6},{8,9},{9,8},{10,11... | collective-permute-start | bytes 688136 | tf_op jit(solution)/shard_map/ppermute | solution.py:256
  91.0 16.3 %collective-permute-start.11 = (bf16[32,1280]{1,0:T(8,128)(2,1)S(1)}, bf16[32,1280]{1,0:T(8,128)(2,1)S(1)}, u32[]{:S(2)}, u32[]{:S(2)}) collective-permute-start(bf16[32,1280]{1,0:T(8,128)(2,1)S(1)} %dynamic-slice_convert_fusion.1), channel_id=1, source_target_pairs={{0,2},{1,3},{2,0},{3,1},{4,6},{5,7},{6,4},{7,5},{8,10},{9,11},{10,... | collective-permute-start | bytes 245768 | tf_op jit(solution)/shard_map/ppermute | solution.py:256
  103.0 11.9 %collective-permute-start.8 = (bf16[32,1792]{1,0:T(8,128)(2,1)S(1)}, bf16[32,1792]{1,0:T(8,128)(2,1)S(1)}, u32[]{:S(2)}, u32[]{:S(2)}) collective-permute-start(bf16[32,1792]{1,0:T(8,128)(2,1)S(1)} %dynamic-slice_convert_fusion), channel_id=1, source_target_pairs={{0,2},{1,3},{2,0},{3,1},{4,6},{5,7},{6,4},{7,5},{8,10},{9,11},{10,... | collective-permute-start | bytes 344072 | tf_op jit(solution)/shard_map/ppermute | solution.py:256
  107.3 13.1 %collective-permute-start.12 = (bf16[16,1280]{1,0:T(8,128)(2,1)S(1)}, bf16[16,1280]{1,0:T(8,128)(2,1)S(1)}, u32[]{:S(2)}, u32[]{:S(2)}) collective-permute-start(bf16[16,1280]{1,0:T(8,128)(2,1)S(1)} %dynamic-slice_convert_fusion.3), channel_id=1, source_target_pairs={{0,4},{1,5},{2,6},{3,7},{4,0},{5,1},{6,2},{7,3},{8,12},{9,13},{10,... | collective-permute-start | bytes 122888 | tf_op jit(solution)/shard_map/ppermute | solution.py:256
  115.0 10.2 %collective-permute-start.9 = (bf16[16,1792]{1,0:T(8,128)(2,1)S(1)}, bf16[16,1792]{1,0:T(8,128)(2,1)S(1)}, u32[]{:S(2)}, u32[]{:S(2)}) collective-permute-start(bf16[16,1792]{1,0:T(8,128)(2,1)S(1)} %dynamic-slice_convert_fusion.2), channel_id=1, source_target_pairs={{0,4},{1,5},{2,6},{3,7},{4,0},{5,1},{6,2},{7,3},{8,12},{9,13},{10,... | collective-permute-start | bytes 172040 | tf_op jit(solution)/shard_map/ppermute | solution.py:256
